TPU v7x, 32 devices: a whole 2x2x4 slice. The times are simulated.
32 devices in a mesh: seq: 8 (over y, x, core), head: 4 (over z).
Axes of the slice: x: 2, y: 2, z: 4, core: 2. Of those that a mesh axis runs over, the one named last changes fastest.
Arguments:
- x_raw: bfloat16 [4096, 4096], P('seq', 'head'), may hold values from -6 to 6
- bc_raw: bfloat16 [4096, 256], P('seq'), may hold values from -6 to 6
- dt_raw: float32 [4096, 64], P('seq', 'head')
- conv_x: float32 [4, 4096], P(None, 'head'), may hold values from -3 to 3
- conv_bc: float32 [4, 256], replicated, may hold values from -3 to 3
- dt_bias: float32 [64], P('head')
- a_log: float32 [64], P('head'), may hold values from 0 to 2.1
- skip_d: float32 [64], P('head'), may hold values from 0.5 to 2
- d_out: bfloat16 [4096, 4096], P('seq', 'head'), may hold values from -6 to 6
Outputs:
- layer_out: bfloat16 [4096, 4096], P('seq', 'head')
- grad_x: bfloat16 [4096, 4096], P('seq', 'head')
- grad_bc: float32 [4096, 256], P('seq')
- grad_steps: float32 [4096, 64], P('seq', 'head')
- grad_conv_x: float32 [4, 4096], P(None, 'head')
- grad_conv_bc: float32 [4, 256], replicated
- grad_bias: float32 [64], P('head')
- grad_rates: float32 [64], P('head')
- grad_skip: float32 [64], P('head')
All inputs are finite; a program needn't handle non-finite values.
Results may differ from a plain program's by a relative error of at most 0.001.
Values may be sent and summed in bfloat16 or wider, within the bound.
A program may use at most 128 MiB of HBM per device.

v0:
```python
import jax
import jax.numpy as jnp
from jax import lax
from jax.sharding import PartitionSpec as P

P_SIZE = 64
N = 128
BLOCK = 128


def shifted(block, axis, distance):
    devices = range(lax.axis_size(axis))
    route = [(i - distance, i) for i in devices if i - distance in devices]
    return lax.ppermute(block, axis, route)


def carried_in(x, axis, combine, identity, reverse):
    size, here = (lax.axis_size(axis), lax.axis_index(axis))
    everything = jax.tree.map(lambda part: lax.all_gather(part, axis), x)
    start = jax.tree.map(
        lambda part, zero: jnp.broadcast_to(jnp.asarray(zero, part.dtype), part.shape), x, identity
    )

    def lap(k, before):
        at = size - 1 - k if reverse else k
        reached = at > here if reverse else at < here
        new = combine(before, jax.tree.map(lambda part: part[at], everything))
        return jax.tree.map(lambda a, b: jnp.where(reached, a, b), new, before)

    return lax.fori_loop(0, size, lap, start)


def conv_pre(padded, taps):
    frames = padded.shape[0] - taps.shape[0] + 1
    total = taps[0] * padded[0:frames].astype(jnp.float32)
    for offset in range(1, taps.shape[0]):
        total = total + taps[offset] * padded[offset : offset + frames].astype(jnp.float32)
    return total


def conv_back(padded, taps, pre_grad):
    margin = taps.shape[0] - 1
    frames = pre_grad.shape[0]
    spread = jnp.pad(pre_grad, ((margin, margin), (0, 0)))
    ext_grad = taps[0] * spread[margin : margin + frames + margin]
    for offset in range(1, margin + 1):
        ext_grad = (
            ext_grad + taps[offset] * spread[margin - offset : margin - offset + frames + margin]
        )
    tap_grad = jnp.stack(
        [
            jnp.sum(pre_grad * padded[offset : offset + frames].astype(jnp.float32), axis=0)
            for offset in range(margin + 1)
        ]
    )
    return (ext_grad, tap_grad)


def silu_slope(pre):
    gate = jax.nn.sigmoid(pre)
    return gate * (1.0 + pre * (1.0 - gate))


def block_terms(x_act, b_proj, step_size, log_decay):
    frames, width = x_act.shape
    head_count = step_size.shape[1]
    num_blocks = frames // BLOCK
    running = jnp.cumsum(log_decay.reshape(num_blocks, BLOCK, head_count), axis=1)
    to_end = jnp.exp(running[:, -1:, :] - running)
    scaled = (
        x_act.reshape(num_blocks, BLOCK, head_count, width // head_count)
        * (step_size.reshape(num_blocks, BLOCK, head_count) * to_end)[..., None]
    )
    block_states = jnp.einsum(
        "kqn,kqhp->khpn",
        b_proj.reshape(num_blocks, BLOCK, -1),
        scaled,
        precision=lax.Precision.HIGHEST,
    )
    return (running, block_states)


def block_mix(block_states, running, state_in):
    block_log = running[:, -1, :]
    totals = jnp.concatenate(
        [jnp.zeros((1, block_log.shape[1]), jnp.float32), jnp.cumsum(block_log, axis=0)], axis=0
    )
    count = totals.shape[0]
    later = jnp.arange(count)[:, None] >= jnp.arange(count)[None, :]
    log_gaps = totals[:, None, :] - totals[None, :, :]
    decay_mat = jnp.exp(jnp.where(later[:, :, None], log_gaps, -jnp.inf))
    stacked = jnp.concatenate([state_in[None], block_states], axis=0)
    mixed = jnp.einsum("zch,chpn->zhpn", decay_mat, stacked, precision=lax.Precision.HIGHEST)
    return (mixed[:-1], mixed[-1], totals)


def emit(x_act, b_proj, c_proj, step_size, running, block_states, skip_d, state_in):
    frames, width = x_act.shape
    head_count = step_size.shape[1]
    num_blocks = frames // BLOCK
    state_heads, state_out, totals = block_mix(block_states, running, state_in)
    x_blocks = x_act.reshape(num_blocks, BLOCK, head_count, width // head_count)
    b_blocks = b_proj.reshape(num_blocks, BLOCK, -1)
    c_blocks = c_proj.reshape(num_blocks, BLOCK, -1)
    step_heads = jnp.transpose(step_size.reshape(num_blocks, BLOCK, head_count), (0, 2, 1))
    running_heads = jnp.transpose(running, (0, 2, 1))
    scores = jnp.einsum("kin,kjn->kij", c_blocks, b_blocks, precision=lax.Precision.HIGHEST)
    causal = jnp.arange(BLOCK)[:, None] >= jnp.arange(BLOCK)[None, :]
    log_gaps = running_heads[:, :, :, None] - running_heads[:, :, None, :]
    decay_mat = jnp.exp(jnp.where(causal[None, None, :, :], log_gaps, -jnp.inf))
    weights = scores[:, None, :, :] * decay_mat * step_heads[:, :, None, :]
    y_diag = jnp.einsum("khij,kjhp->kihp", weights, x_blocks, precision=lax.Precision.HIGHEST)
    y_carry = (
        jnp.einsum("kin,khpn->kihp", c_blocks, state_heads, precision=lax.Precision.HIGHEST)
        * jnp.exp(running)[..., None]
    )
    y_full = y_diag + y_carry + skip_d[None, None, :, None] * x_blocks
    return (y_full.reshape(frames, width), state_out)


def link_states(earlier, later):
    return (earlier[0] * later[0], later[0][:, None, None] * earlier[1] + later[1])


def local(x_raw, bc_raw, dt_raw, conv_x, conv_bc, dt_bias, a_log, skip_d, d_out):
    margin = conv_x.shape[0] - 1
    frames, width = x_raw.shape
    head_count = dt_raw.shape[1]
    num_blocks = frames // BLOCK
    tails = jnp.concatenate([x_raw[-margin:], bc_raw[-margin:]], axis=1)
    before = shifted(tails, "seq", 1)
    x_ext = jnp.concatenate([before[:, :width], x_raw], axis=0)
    bc_ext = jnp.concatenate([before[:, width:], bc_raw], axis=0)
    x_pre = conv_pre(x_ext, conv_x)
    x_act = jax.nn.silu(x_pre)
    bc_pre = conv_pre(bc_ext, conv_bc)
    bc_act = jax.nn.silu(bc_pre)
    b_proj = bc_act[:, :N]
    c_proj = bc_act[:, N:]
    raw_sum = dt_raw + dt_bias
    step_size = jax.nn.softplus(raw_sum)
    rates = jnp.exp(a_log)
    log_decay = -step_size * rates
    (running, block_states), pull_terms = jax.vjp(block_terms, x_act, b_proj, step_size, log_decay)
    zero_state = jnp.zeros((head_count, P_SIZE, N), jnp.float32)
    unused, local_out, totals = block_mix(block_states, running, zero_state)
    log_total = totals[-1]
    decay_total = jnp.exp(log_total)
    unused_decay, state_in = carried_in(
        (decay_total, local_out),
        "seq",
        link_states,
        (jnp.ones_like(decay_total), zero_state),
        False,
    )
    (y_full, state_out), pull_emit = jax.vjp(
        emit, x_act, b_proj, c_proj, step_size, running, block_states, skip_d, state_in
    )
    layer_out = y_full.astype(jnp.bfloat16)
    grad_y = d_out.astype(jnp.float32)
    reach = jnp.exp(totals[:-1][:, None, :] + running)
    local_grad = jnp.einsum(
        "kqh,kqn,kqhp->hpn",
        reach,
        c_proj.reshape(num_blocks, BLOCK, N),
        grad_y.reshape(num_blocks, BLOCK, head_count, P_SIZE),
        precision=lax.Precision.HIGHEST,
    )
    unused_back, grad_state = carried_in(
        (decay_total, local_grad),
        "seq",
        link_states,
        (jnp.ones_like(decay_total), zero_state),
        True,
    )
    g_x_emit, g_b_emit, g_c, g_step_emit, g_running, g_states, skip_part, unused_state = pull_emit(
        (grad_y, grad_state)
    )
    g_x_terms, g_b_terms, g_step_terms, g_log = pull_terms((g_running, g_states))
    g_x = g_x_emit + g_x_terms
    g_step = g_step_emit + g_step_terms
    bc_local = jnp.concatenate([g_b_emit + g_b_terms, g_c], axis=1)
    bc_grad = lax.psum(bc_local, "head")
    bc_ext_grad, conv_bc_grad = conv_back(bc_ext, conv_bc, bc_grad * silu_slope(bc_pre))
    x_ext_grad, conv_x_grad = conv_back(x_ext, conv_x, g_x * silu_slope(x_pre))
    heads_back = jnp.concatenate([x_ext_grad[:margin], bc_ext_grad[:margin]], axis=1)
    after = shifted(heads_back, "seq", -1)
    grad_x = x_ext_grad[margin:].at[-margin:].add(after[:, :width]).astype(jnp.bfloat16)
    grad_bc = bc_ext_grad[margin:].at[-margin:].add(after[:, width:])
    grad_steps = (g_step - g_log * rates) * jax.nn.sigmoid(raw_sum)
    summed = lax.psum(
        (
            conv_x_grad,
            conv_bc_grad,
            jnp.sum(grad_steps, axis=0),
            jnp.sum(g_log * log_decay, axis=0),
            skip_part,
        ),
        "seq",
    )
    return (
        layer_out,
        grad_x,
        grad_bc,
        grad_steps,
        summed[0],
        summed[1],
        summed[2],
        summed[3],
        summed[4],
    )


def solution(mesh):
    placed = (
        P("seq", "head"),
        P("seq", None),
        P("seq", "head"),
        P(None, "head"),
        P(),
        P("head"),
        P("head"),
        P("head"),
        P("seq", "head"),
    )
    return jax.shard_map(
        local,
        mesh=mesh,
        in_specs=placed,
        out_specs=(
            P("seq", "head"),
            P("seq", "head"),
            P("seq", None),
            P("seq", "head"),
            P(None, "head"),
            P(),
            P("head"),
            P("head"),
            P("head"),
        ),
        check_vma=False,
    )
```

profile of v0, /device:TPU:0, one launch (start us, length us, event | category | flops | bytes accessed | tf_op | source)
XLA Modules:
  0.0 275.7 jit_solution(17738351458266476436)
XLA Ops:
  9.7 3.1 %collective-permute-start = (bf16[3,1280]{0,1:T(8,128)(2,1)}, bf16[3,1280]{0,1:T(8,128)(2,1)}, u32[]{:S(2)}, u32[]{:S(2)}) collective-permute-start(bf16[3,1280]{0,1:T(8,128)(2,1)} %copy.268), channel_id=1, source_target_pairs={{0,4},{4,8},{8,12},{12,16},{16,20},{20,24},{24,28},{1,5},{5,9},{9,... | collective-permute-start | bytes 23048 | tf_op jit(solution)/shard_map/ppermute | solution.py:14
  21.5 2.6 fusion.86
  30.0 11.0 %all-gather.1 = f32[8,1,16]{2,1,0:T(1,128)} all-gather(f32[1,1,16]{2,1,0:T(1,128)S(1)} %exponential_bitcast_fusion), channel_id=1, replica_groups=mesh['seq'=8,'head'=4] {'seq'}, dimensions={0}, use_global_device_ids=true | all-gather | bytes 576 | tf_op jit(solution)/shard_map/all_gather | solution.py:19
  43.2 4.5 %multiply_reduce_fusion.1 = (f32[1024]{0:T(1024)}, f32[512,1024]{0,1:T(8,128)}, f32[512,1024]{0,1:T(8,128)}) fusion(bf16[512,1024]{0,1:T(8,128)(2,1)S(1)} %copy.289, bf16[512,1024]{0,1:T(8,128)(2,1)S(1)} %copy.269, f32[1024]{0:T(1024)S(1)} %bitcast.208, bf16[3,1024]{0,1:T(8,128)(2,1)S(1)} %slice.214, f32[1024]{0:T(1024)S(1)} %bitcast.210, ...), kind=kLoop, calls=%fused_computation.66 | loop fusion | flops 14154752 | bytes 6318080 | tf_op jit(solution)/shard_map/transpose(jvp())/reduce_sum | solution.py:117
  50.5 5.0 %fusion.70 = f32[4,16,64,128]{3,2,1,0:T(8,128)} fusion(f32[4,128,128,1]{2,1,3,0:T(8,128)S(1)} %bitcast.186, f32[4,128,16,64]{1,0,3,2:T(4,128)} %reshape.206, f32[4,128,16]{1,2,0:T(8,128)S(1)} %exp.58), kind=kOutput, calls=%fused_computation.93 | convolution fusion | flops 805830656 | bytes 4489216 | tf_op jit(solution)/shard_map/transpose(jvp(kin,khpn->kihp))/dot_general | solution.py:114
  55.5 6.5 %fusion.26 = (f32[4,16,128]{2,1,0:T(8,128)}, f32[4,16,128]{2,1,0:T(8,128)}, f32[4,16,128]{2,1,0:T(8,128)}, f32[4,128,128]{2,1,0:T(8,128)}) fusion(f32[4,16,128]{2,1,0:T(8,128)S(1)} %copy-done.39, f32[4,16,128]{2,1,0:T(8,128)S(1)} %copy-done.36, f32[4,128,128]{2,1,0:T(8,128)S(1)} %fusion.172, pred[128,128]{1,0:T(8,128)(4,1)S(1)} %copy-done.45, ...), kind=kOutput, calls=%fused_computation.47 | convolution fusion | flops 818847744 | bytes 3850240 | tf_op jit(solution)/shard_map/transpose(jvp(khij,kjhp->kihp))/dot_general | solution.py:112
  62.9 15.3 %while.33 = (s32[]{:T(128)}, f32[16,64,128]{2,1,0:T(8,128)S(1)}, s32[]{:T(128)}, f32[8,16]{1,0:T(8,128)}, f32[8,16,64,128]{3,2,1,0:T(8,128)}, /*index=5*/s32[]{:T(128)}, s32[]{:T(128)}, s32[]{:T(128)}, s32[]{:T(128)}) while((s32[]{:T(128)}, f32[16,64,128]{2,1,0:T(8,128)S(1)}, s32[]{:T(128)}, f32[8,16]{1,0:T(8,128)}, ...), condition=%wide.region_5.6_spmd.clone, body=%wide.region_4.5_spmd.clone.sunk | while | flops 524296 | bytes 1573231 | solution.py:30
  80.0 5.1 %fusion.33 = f32[5,16,64,128]{3,0,2,1:T(8,128)S(1)} fusion(f32[16,64,128,5]{2,1,0,3:T(8,128)S(1)} %add_bitcast_fusion, f32[5,16]{0,1:T(8,128)S(1)} %concatenate.33.clone, pred[5,5]{1,0:T(8,128)(4,1)S(1)} %copy-done.54), kind=kOutput, calls=%fused_computation.50 | convolution fusion | flops 39322400 | bytes 5243225 | tf_op jit(solution)/shard_map/transpose(jvp(zch,chpn->zhpn))/dot_general | solution.py:93
  87.0 3.3 %multiply_reduce_fusion.3 = (f32[4,128,16]{1,2,0:T(8,128)S(1)}, f32[4,128,16,64]{1,3,2,0:T(8,128)}) fusion(f32[4,128,16,64]{1,0,3,2:T(4,128)S(1)} %copy-done.1, f32[4,128,128,1]{2,1,3,0:T(8,128)S(1)} %bitcast.191, f32[4,16,64,128]{3,0,2,1:T(4,128)S(1)} %split.8), kind=kOutput, calls=%fused_computation.68 | convolution fusion | flops 806346752 | bytes 6586368 | tf_op jit(solution)/shard_map/transpose(jvp(kqn,kqhp->khpn))/dot_general | solution.py:74
  96.3 15.8 %fusion.27 = f32[5,16,64,128]{3,0,2,1:T(8,128)S(1)} fusion(f32[4,16,64,128]{3,0,2,1:T(4,128)S(1)} %copy.338, f32[5,16]{0,1:T(8,128)S(1)} %concatenate.33.clone, pred[5,5]{1,0:T(8,128)(4,1)S(1)} %copy-done.54), kind=kOutput, calls=%fused_computation.48 | convolution fusion | flops 39322400 | bytes 4718937 | tf_op jit(solution)/shard_map/zch,chpn->zhpn/dot_general | solution.py:93
  116.2 5.3 %fusion.43 = f32[4,128,16,64]{1,3,2,0:T(8,128)S(1)} fusion(f32[4,128,16,64]{1,3,2,0:T(8,128)} %get-tuple-element.418, f32[4,128,16,64]{1,0,3,2:T(4,128)} %reshape.206, f32[4,16,128]{2,1,0:T(8,128)} %copy.275, f32[4,16,128]{2,1,0:T(8,128)S(1)} %copy-done.37, f32[4,128,128]{2,1,0:T(8,128)} %copy-done.24, pred[128,128]{1,0:T(8,128)(4,1)} %iota_compare_fusion, ...), kind=kOutput, calls=%fused_computation.60 | convolution fusion | flops 811597824 | bytes 7716928 | tf_op jit(solution)/shard_map/transpose(jvp(khij,kjhp->kihp))/dot_general | solution.py:112
  121.5 2.7 copy.299
  124.9 6.9 %fusion.39 = (f32[1024]{0:T(1024)S(1)}, f32[1024]{0:T(1024)S(1)}, f32[1024]{0:T(1024)S(1)}, f32[1024]{0:T(1024)S(1)}, f32[512,1024]{0,1:T(8,128)S(1)}) fusion(bf16[512,1024]{0,1:T(8,128)(2,1)} %copy-done.6, bf16[3,1024]{0,1:T(8,128)(2,1)} %copy-done.14, f32[512,1024]{0,1:T(8,128)} %get-tuple-element.393, f32[128,8,4,128]{3,2,1,0:T(4,128)} %bitcast.189), kind=kLoop, calls=%fused_computation.54 | loop fusion | flops 15200256 | bytes 7362560 | tf_op jit(solution)/shard_map/reduce_sum | solution.py:52
  131.9 2.9 %fusion.21 = f32[515,1024]{0,1:T(8,128)S(1)} fusion(f32[512,1024]{0,1:T(8,128)S(1)} %get-tuple-element.397, f32[1024]{0:T(1024)S(1)} %bitcast.209, f32[1024]{0:T(1024)S(1)} %bitcast.211, f32[1024]{0:T(1024)S(1)} %bitcast.207, f32[1024]{0:T(1024)S(1)} %bitcast.205), kind=kLoop, calls=%fused_computation.40 | loop fusion | flops 3691520 | bytes 4222976 | tf_op jit(solution)/shard_map/add | solution.py:48
  141.6 5.9 %fusion.94 = f32[4,128,128]{2,1,0:T(8,128)S(1)} fusion(f32[4,16,64,128]{3,0,2,1:T(4,128)} %copy-done.4, f32[4,128,16,64]{1,0,3,2:T(4,128)} %copy-done, f32[4,128,16]{1,2,0:T(8,128)S(1)} %get-tuple-element.407), kind=kOutput, calls=%fused_computation.111 | convolution fusion | flops 805830656 | bytes 4489216 | tf_op jit(solution)/shard_map/transpose(jvp(kqn,kqhp->khpn))/dot_general | solution.py:74
  150.3 15.4 %while.32 = (s32[]{:T(128)}, f32[16,64,128]{2,1,0:T(8,128)S(1)}, s32[]{:T(128)}, f32[8,16]{1,0:T(8,128)}, f32[8,16,64,128]{3,2,1,0:T(8,128)}, /*index=5*/s32[]{:T(128)}, s32[]{:T(128)}) while((s32[]{:T(128)}, f32[16,64,128]{2,1,0:T(8,128)S(1)}, s32[]{:T(128)}, f32[8,16]{1,0:T(8,128)}, f32[8,16,64,128]{3,2,1,0:T(8,128)}, ...), condition=%wide.region_3.4_spmd.clone, body=%wide.region_2.3_spmd.clone.sunk | while | flops 524292 | bytes 1573169 | solution.py:30
  167.6 13.4 %fusion.160 = (f32[5,16]{0,1:T(8,128)S(1)}, f32[5,16]{0,1:T(8,128)S(1)}) fusion(f32[5,16]{0,1:T(8,128)S(1)} %concatenate.33.clone, f32[5,16,64,128]{3,2,1,0:T(8,128)S(1)} %pad_maximum_fusion, f32[16,64,128,5]{2,1,0,3:T(8,128)S(1)} %add_bitcast_fusion, pred[5,5]{1,0:T(8,128)(4,1)S(1)} %copy-done.55), kind=kOutput, calls=%fused_computation.202 | convolution fusion | flops 39323840 | bytes 5243865 | tf_op jit(solution)/shard_map/transpose(jvp(zch,chpn->zhpn))/dot_general | solution.py:93
  181.0 5.2 %fusion.30 = f32[5,16,64,128]{3,0,2,1:T(8,128)S(1)} fusion(f32[5,16,64,128]{3,2,1,0:T(8,128)S(1)} %pad_maximum_fusion, f32[5,16]{0,1:T(8,128)S(1)} %concatenate.33.clone, pred[5,5]{1,0:T(8,128)(4,1)S(1)} %copy-done.55), kind=kOutput, calls=%fused_computation.49 | convolution fusion | flops 39322400 | bytes 5243225 | tf_op jit(solution)/shard_map/jvp(zch,chpn->zhpn)/dot_general | solution.py:93
  187.9 3.6 %fusion.89 = f32[4,128,128]{2,1,0:T(8,128)S(1)} fusion(f32[4,16,64,128]{3,0,2,1:T(4,128)S(1)} %slice.228, f32[4,128,16,64]{1,0,3,2:T(4,128)S(1)} %copy-done.3, f32[4,128,16]{1,2,0:T(8,128)S(1)} %exp.58), kind=kOutput, calls=%fused_computation.110 | convolution fusion | flops 805830656 | bytes 4489216 | tf_op jit(solution)/shard_map/transpose(jvp(kin,khpn->kihp))/dot_general | solution.py:114
  191.5 3.3 %multiply_reduce_fusion.2 = (f32[4,128,16]{1,2,0:T(8,128)S(1)}, f32[4,128,16,64]{1,3,2,0:T(8,128)}) fusion(f32[4,128,16,64]{1,0,3,2:T(4,128)S(1)} %copy-done.3, f32[4,128,128,1]{2,1,3,0:T(8,128)S(1)} %bitcast.188, f32[4,16,64,128]{3,0,2,1:T(4,128)S(1)} %slice.228), kind=kOutput, calls=%fused_computation.67 | convolution fusion | flops 806346752 | bytes 6586368 | tf_op jit(solution)/shard_map/jvp(kin,khpn->kihp)/dot_general | solution.py:114
  198.0 4.6 %reduce_window_sum.52 = f32[4,128,16]{2,1,0:T(8,128)S(1)} reduce-window(f32[4,128,16]{2,1,0:T(8,128)S(1)} %copy.317, f32[]{:T(128)} %constant.150.clone.1), window={size=1x128x1 pad=0_0x0_127x0_0}, to_apply=%region_17.18 | reduce-window | flops 1040384 | bytes 65540 | tf_op jit(solution)/shard_map/transpose(jvp(jit(cumsum)))/reduce_window_sum | solution.py:68
  202.8 9.8 %fusion.45 = bf16[4,128,16,64]{1,3,2,0:T(8,128)(2,1)S(1)} fusion(f32[4,128,16,64]{1,3,2,0:T(8,128)} %get-tuple-element.420, f32[4,16,128]{2,1,0:T(8,128)} %copy.275, f32[4,16,128]{2,1,0:T(8,128)} %copy.273, f32[4,128,128]{2,1,0:T(8,128)S(1)} %copy-done.25, pred[128,128]{1,0:T(8,128)(4,1)} %iota_compare_fusion, f32[4,128,16,64]{1,0,3,2:T(4,128)S(1)} %copy-done.2, ...), kind=kOutput, calls=%fused_computation.63 | convolution fusion | flops 812122112 | bytes 5619776 | tf_op jit(solution)/shard_map/jvp(khij,kjhp->kihp)/dot_general | solution.py:112
  217.6 17.9 %all-reduce.11.cloned.1.call-done = f32[512,256]{1,0:T(8,128)} async-done(((f32[512,256]{1,0:T(8,128)}), f32[512,256]{1,0:T(8,128)}) %all-reduce.11.cloned.1.call-update) | async-done | bytes 524304 | tf_op jit(solution)/shard_map/psum | solution.py:183
  238.8 25.9 %all-reduce.8 = (f32[4,1024]{1,0:T(4,128)}, f32[4,256]{1,0:T(4,128)}, f32[16]{0:T(128)}, f32[16]{0:T(128)}, f32[16]{0:T(128)}) all-reduce(f32[4,1024]{1,0:T(4,128)S(1)} %copy-done.31, f32[4,256]{1,0:T(4,128)S(1)} %pad_maximum_fusion.7, f32[16]{0:T(128)S(1)} %get-tuple-element.394, ...), channel_id=1, replica_groups=mesh['seq'=8,'head'=4] {'seq'}, use_global_device_ids=true, to_apply=%region_22.23 | all-reduce | flops 5168 | bytes 41344 | tf_op jit(solution)/shard_map/psum | solution.py:191
  (248 shorter events, 95.3 us)
Async XLA Ops:
  7.2 8.8 %copy-start.17 = (bf16[512,1024]{1,0:T(8,128)(2,1)S(1)}, bf16[512,1024]{1,0:T(8,128)(2,1)}, u32[]{:S(2)}) copy-start(bf16[512,1024]{1,0:T(8,128)(2,1)} %param.25) | copy-start | bytes 3145732
  7.2 55.7 %all-gather.7.cloned.1.call-start = ((), (), s32[]{:S(2)}) async-start(), calls=%async_computation.2 | async-start | bytes 4718592 | tf_op jit(solution)/shard_map/all_gather | solution.py:19
  9.7 9.8 %collective-permute-start = (bf16[3,1280]{0,1:T(8,128)(2,1)}, bf16[3,1280]{0,1:T(8,128)(2,1)}, u32[]{:S(2)}, u32[]{:S(2)}) collective-permute-start(bf16[3,1280]{0,1:T(8,128)(2,1)} %copy.268), channel_id=1, source_target_pairs={{0,4},{4,8},{8,12},{12,16},{16,20},{20,24},{24,28},{1,5},{5,9},{9,... | collective-permute-start | bytes 23048 | tf_op jit(solution)/shard_map/ppermute | solution.py:14
  24.2 126.1 %all-gather.5.cloned.1.call-start = ((), (), s32[]{:S(2)}) async-start(), calls=%async_computation | async-start | bytes 4718592 | tf_op jit(solution)/shard_map/all_gather | solution.py:19
  26.9 16.4 %copy-start.6 = (bf16[512,1024]{0,1:T(8,128)(2,1)}, bf16[512,1024]{0,1:T(8,128)(2,1)S(1)}, u32[]{:S(2)}) copy-start(bf16[512,1024]{0,1:T(8,128)(2,1)S(1)} %copy.269) | copy-start | bytes 3145732
  26.9 15.3 %copy-start.44 = (f32[4,1024]{1,0:T(4,128)S(1)}, f32[4,1024]{1,0:T(4,128)}, u32[]{:S(2)}) copy-start(f32[4,1024]{1,0:T(4,128)} %param.20) | copy-start | bytes 49156
  96.3 19.9 %copy-start.37 = (f32[4,16,128]{2,1,0:T(8,128)S(1)}, f32[4,16,128]{2,1,0:T(8,128)}, u32[]{:S(2)}) copy-start(f32[4,16,128]{2,1,0:T(8,128)} %copy.273) | copy-start | bytes 98308
  113.4 122.0 %all-reduce.11.cloned.1.call-start = ((), (), s32[]{:S(2)}) async-start(), calls=%async_computation.1 | async-start | bytes 1048576 | tf_op jit(solution)/shard_map/psum | solution.py:183
  124.9 7.0 %copy-start.35 = (f32[1,1024]{1,0:T(1,128)S(1)}, f32[1,1024]{1,0:T(1,128)}, u32[]{:S(2)}) copy-start(f32[1,1024]{1,0:T(1,128)} %copy-done.34) | copy-start | bytes 12292
  194.8 8.0 %copy-start.2 = (f32[4,128,16,64]{1,0,3,2:T(4,128)S(1)}, f32[4,128,16,64]{1,0,3,2:T(4,128)}, u32[]{:S(2)}) copy-start(f32[4,128,16,64]{1,0,3,2:T(4,128)} %copy-done) | copy-start | bytes 6291460
  194.8 8.0 %copy-start.25 = (f32[4,128,128]{2,1,0:T(8,128)S(1)}, f32[4,128,128]{2,1,0:T(8,128)}, u32[]{:S(2)}) copy-start(f32[4,128,128]{2,1,0:T(8,128)} %copy-done.24) | copy-start | bytes 786436
  194.8 8.0 %copy-start.62 = (f32[16]{0:T(128)S(1)}, f32[16]{0:T(128)}, u32[]{:S(2)}) copy-start(f32[16]{0:T(128)} %param.24) | copy-start | bytes 196
  214.4 21.1 %copy-start.16 = (bf16[512,256]{1,0:T(8,128)(2,1)S(1)}, bf16[512,256]{1,0:T(8,128)(2,1)}, u32[]{:S(2)}) copy-start(bf16[512,256]{1,0:T(8,128)(2,1)} %param.18) | copy-start | bytes 786436
  214.4 21.1 %copy-start.41 = (bf16[3,256]{1,0:T(4,128)(2,1)S(1)}, bf16[3,256]{1,0:T(4,128)(2,1)}, u32[]{:S(2)}) copy-start(bf16[3,256]{1,0:T(4,128)(2,1)} %copy-done.40) | copy-start | bytes 4612
  214.4 21.1 %copy-start.47 = (f32[1,256]{1,0:T(1,128)S(1)}, f32[1,256]{1,0:T(1,128)}, u32[]{:S(2)}) copy-start(f32[1,256]{1,0:T(1,128)} %copy-done.46) | copy-start | bytes 3076
  214.4 21.1 %copy-start.49 = (f32[1,256]{1,0:T(1,128)S(1)}, f32[1,256]{1,0:T(1,128)}, u32[]{:S(2)}) copy-start(f32[1,256]{1,0:T(1,128)} %copy-done.48) | copy-start | bytes 3076
  214.4 21.1 %copy-start.51 = (f32[1,256]{1,0:T(1,128)S(1)}, f32[1,256]{1,0:T(1,128)}, u32[]{:S(2)}) copy-start(f32[1,256]{1,0:T(1,128)} %copy-done.50) | copy-start | bytes 3076
  214.4 21.1 %copy-start.53 = (f32[1,256]{1,0:T(1,128)S(1)}, f32[1,256]{1,0:T(1,128)}, u32[]{:S(2)}) copy-start(f32[1,256]{1,0:T(1,128)} %copy-done.52) | copy-start | bytes 3076
  214.4 22.9 %copy-start.30 = (f32[3,1024]{1,0:T(4,128)S(1)}, f32[3,1024]{1,0:T(4,128)}, u32[]{:S(2)}) copy-start(f32[3,1024]{1,0:T(4,128)} %copy.305) | copy-start | bytes 36868
  216.7 22.0 %copy-start.31 = (f32[4,1024]{1,0:T(4,128)S(1)}, f32[4,1024]{1,0:T(4,128)}, u32[]{:S(2)}) copy-start(f32[4,1024]{1,0:T(4,128)} %pad_maximum_fusion.5) | copy-start | bytes 49156
  216.7 22.0 %copy-start.58 = (f32[16]{0:T(128)S(1)}, f32[16]{0:T(128)}, u32[]{:S(2)}) copy-start(f32[16]{0:T(128)} %reduce_sum.244) | copy-start | bytes 196
  216.7 47.9 %copy-start.29 = (f32[3,1024]{1,0:T(4,128)S(1)}, f32[3,1024]{1,0:T(4,128)}, u32[]{:S(2)}) copy-start(f32[3,1024]{1,0:T(4,128)} %copy.306) | copy-start | bytes 36868
  216.7 48.2 %copy-start.13 = (bf16[512,1024]{0,1:T(8,128)(2,1)S(1)}, bf16[512,1024]{0,1:T(8,128)(2,1)}, u32[]{:S(2)}) copy-start(bf16[512,1024]{0,1:T(8,128)(2,1)} %slice.229) | copy-start | bytes 3145732
  237.4 27.3 %collective-permute-start.1 = (f32[3,1280]{1,0:T(4,128)S(1)}, f32[3,1280]{1,0:T(4,128)S(1)}, u32[]{:S(2)}, u32[]{:S(2)}) collective-permute-start(f32[3,1280]{1,0:T(4,128)S(1)} %pad_maximum_fusion.4), channel_id=1, source_target_pairs={{4,0},{8,4},{12,8},{16,12},{20,16},{24,20},{28,24},{5,1},{9,5},{13... | collective-permute-start | bytes 46088 | tf_op jit(solution)/shard_map/ppermute | solution.py:14
  (44 other events, 145.0 us)
Sparse Core Ops, SparseCore 0:
  24.3 38.5 all-gather.6
  113.5 36.7 all-gather.4
  197.1 38.2 all-reduce.10
where the time goes:
time: 280 us; the launch traced here: 276 us
  matrix products  89.2 us (32%)
  local copies, waits for them, and re-layouts  54.6 us (20%)
  other arithmetic  54.3 us (19%)
  blocking collectives  36.9 us (13%)
  waiting for transfers between devices  20.3 us (7%)
  between operations  14.9 us (5%)
  starting transfers between devices  4.49 us (2%)
    dot_general x4, matrix products, block_mix(): jnp.einsum('zch,chpn->zhpn', decay_mat, stacked, precision=lax.Precision....  39.6 us
    psum x1, blocking collectives, local(): lax.psum((conv_x_grad, conv_bc_grad, jnp.sum(grad_steps, axis=0), jnp.sum...  25.9 us
    dot_general x3, matrix products, emit(): jnp.einsum('khij,kjhp->kihp', weights, x_blocks, precision=lax.Precision....  21.7 us
    select_n x16, other arithmetic, lap(): return jax.tree.map(lambda a, b: jnp.where(reached, a, b), new, before)  18.7 us
    psum x1, waiting for transfers between devices, local(): bc_grad = lax.psum(bc_local, 'head')  17.9 us
    unnamed x134, local copies, waits for them, and re-layouts  14.7 us
    dot_general x3, matrix products, emit(): jnp.einsum('kin,khpn->kihp', c_blocks, state_heads, precision=lax.Precisi...  11.9 us
    dot_general x3, matrix products, block_terms(): jnp.einsum('kqn,kqhp->khpn', b_proj.reshape(num_blocks, BLOCK, -1), scale...  11.1 us
  transfers between devices with their start and end apart: 5, of which 3 were waited for; matrix products, arithmetic and copies ran while one was open for 32% of the time, Pallas kernels for 0%

commit v1 on v0

v1 whole, which is shorter than its diff:
```python
import jax
import jax.numpy as jnp
from jax import lax
from jax.experimental import pallas as pl
from jax.experimental.pallas import tpu as pltpu
from jax.sharding import PartitionSpec as P

P_SIZE = 64
N = 128
BLOCK = 128
LANES = 128
F32 = jnp.float32
BF16 = jnp.bfloat16
NN = (((1,), (0,)), ((), ()))
NT = (((1,), (1,)), ((), ()))
TN = (((0,), (0,)), ((), ()))
MESH = pl.DeviceIdType.MESH
VMEM_LIMIT = 44 * 2**20


def shifted(block, axis, distance):
    devices = range(lax.axis_size(axis))
    route = [(i - distance, i) for i in devices if i - distance in devices]
    return lax.ppermute(block, axis, route)


def split(a):
    high = a.astype(BF16)
    return high, (a - high.astype(F32)).astype(BF16)


def mm(a, b, dims=NN):
    return lax.dot_general(a, b, dims, preferred_element_type=F32)


def dot3(a, b, dims=NN):
    return mm(a[0], b[0], dims) + (mm(a[0], b[1], dims) + mm(a[1], b[0], dims))


def exact(a, b, dims=NN):
    return lax.dot_general(
        a, b, dims, precision=lax.Precision.HIGHEST, preferred_element_type=F32
    )


def silu(pre):
    return pre / (1.0 + jnp.exp(-pre))


def lane_ids(shape):
    return lax.broadcasted_iota(jnp.int32, shape, 1)


def row_ids(shape):
    return lax.broadcasted_iota(jnp.int32, shape, 0)


def rows_of(k):
    return slice(k * BLOCK, (k + 1) * BLOCK)


def pair_columns(rolled):
    first = jnp.broadcast_to(rolled[:, 0:1], rolled.shape)
    second = jnp.broadcast_to(rolled[:, 1:2], rolled.shape)
    return jnp.where(lane_ids(rolled.shape) < P_SIZE, first, second)


def conv_x_pre(xp, halo_ref, x_ref, taps_ref):
    frames = x_ref.shape[0]
    xp[0:8, :] = halo_ref[...]
    xp[8 : 8 + frames, :] = x_ref[...].astype(F32)
    pre = taps_ref[0:1, :] * xp[5 : 5 + frames, :]
    for k in range(1, 4):
        pre = pre + taps_ref[k : k + 1, :] * xp[5 + k : 5 + k + frames, :]
    return pre


def terms_kernel(
    halo_ref, x_ref, gy_ref, taps_ref, bc_ref, taps_bc_ref, s_ref, la_ref,
    bs_ref, bg_ref, ls_ref, lg_ref, dec_ref, run_ref, b_ref, c_ref, sc_ref, runt_ref,
    xp, bth, btl, cth, ctl,
):
    p = pl.program_id(0)
    frames = x_ref.shape[0]
    blocks = frames // BLOCK

    @pl.when(p == 0)
    def _():
        square = (BLOCK, BLOCK)
        tril = jnp.where(row_ids(square) >= lane_ids(square), 1.0, 0.0).astype(F32)
        pre = taps_bc_ref[0:1, :] * bc_ref[5 : 5 + frames, :]
        for k in range(1, 4):
            pre = pre + taps_bc_ref[k : k + 1, :] * bc_ref[5 + k : 5 + k + frames, :]
        act = silu(pre)
        b_ref[...] = act[:, :N]
        c_ref[...] = act[:, N:]
        for k in range(blocks):
            run = exact(tril, la_ref[rows_of(k), :])
            run_ref[rows_of(k), :] = run
            runt_ref[k] = run.T
            b = b_ref[rows_of(k), :]
            c = c_ref[rows_of(k), :]
            bth[k], btl[k] = split(b.T)
            cth[k], ctl[k] = split(c.T)
            sc_ref[k] = exact(c, b, NT)

    xa = silu(conv_x_pre(xp, halo_ref, x_ref, taps_ref))
    back = lax.rem(LANES - 2 * p, LANES)
    state = jnp.zeros((N, LANES), F32)
    total = jnp.zeros((1, LANES), F32)
    decays = []
    for k in range(blocks):
        run = pair_columns(pltpu.roll(run_ref[rows_of(k), :], back, 1))
        step = pair_columns(pltpu.roll(s_ref[rows_of(k), :], back, 1))
        tot = run[BLOCK - 1 : BLOCK, :]
        scaled = xa[rows_of(k), :] * (step * jnp.exp(tot - run))
        bs = dot3((bth[k], btl[k]), split(scaled))
        bs_ref[0, k] = bs
        bg_ref[0, k] = dot3(
            (cth[k], ctl[k]), split(gy_ref[rows_of(k), :].astype(F32) * jnp.exp(run))
        )
        decays.append(jnp.exp(tot))
        state = decays[k] * state + bs
        total = total + tot
    ls_ref[0] = state
    grad = jnp.zeros((N, LANES), F32)
    for k in reversed(range(blocks)):
        grad = decays[k] * grad + bg_ref[0, k]
    lg_ref[0] = grad
    dec_ref[0] = jnp.broadcast_to(jnp.exp(total), (8, LANES))


def chain_kernel(
    size, ls_ref, lg_ref, dec_ref, sin_ref, gin_ref,
    fout, fin, bout, bin_, fsend, frecv, bsend, brecv,
):
    me = lax.axis_index("seq")
    chunks = ls_ref.shape[0]
    lag = 2
    barrier = pltpu.get_barrier_semaphore()

    @pl.when(me > 0)
    def _():
        pl.semaphore_signal(barrier, inc=1, device_id={"seq": me - 1}, device_id_type=MESH)

    @pl.when(me < size - 1)
    def _():
        pl.semaphore_signal(barrier, inc=1, device_id={"seq": me + 1}, device_id_type=MESH)

    pl.semaphore_wait(barrier, lax.min(me, 1) + lax.min(size - 1 - me, 1))

    def copy(out, into, send, recv, k, target):
        return pltpu.make_async_remote_copy(
            src_ref=out.at[k],
            dst_ref=into.at[k],
            send_sem=send.at[k],
            recv_sem=recv.at[k],
            device_id={"seq": target},
            device_id_type=MESH,
        )

    def forward(k):
        @pl.when(me == 0)
        def _():
            sin_ref[k] = jnp.zeros((N, LANES), F32)
            fout[k] = ls_ref[k]

        @pl.when(me > 0)
        def _():
            copy(fout, fin, fsend, frecv, k, me - 1).wait_recv()
            got = fin[k]
            sin_ref[k] = got
            fout[k] = dec_ref[k][0:1, :] * got + ls_ref[k]

        @pl.when(me < size - 1)
        def _():
            copy(fout, fin, fsend, frecv, k, me + 1).start()

    def backward(k):
        @pl.when(me == size - 1)
        def _():
            gin_ref[k] = jnp.zeros((N, LANES), F32)
            bout[k] = lg_ref[k]

        @pl.when(me < size - 1)
        def _():
            copy(bout, bin_, bsend, brecv, k, me + 1).wait_recv()
            got = bin_[k]
            gin_ref[k] = got
            bout[k] = dec_ref[k][0:1, :] * got + lg_ref[k]

        @pl.when(me > 0)
        def _():
            copy(bout, bin_, bsend, brecv, k, me - 1).start()

    late_f = lax.max(0, 2 * me - (size - 1)) * lag
    late_b = lax.max(0, (size - 1) - 2 * me) * lag

    def turn(step, carry):
        kf = step - late_f
        kb = step - late_b

        @pl.when(jnp.logical_and(kf >= 0, kf < chunks))
        def _():
            forward(kf)

        @pl.when(jnp.logical_and(kb >= 0, kb < chunks))
        def _():
            backward(kb)

        return carry

    lax.fori_loop(0, chunks + (size - 1) * lag, turn, 0)

    def drain(k, carry):
        @pl.when(me < size - 1)
        def _():
            copy(fout, fin, fsend, frecv, k, me + 1).wait_send()

        @pl.when(me > 0)
        def _():
            copy(bout, bin_, bsend, brecv, k, me - 1).wait_send()

        return carry

    lax.fori_loop(0, chunks, drain, 0)


def main_kernel(
    halo_ref, x_ref, gy_ref, taps_ref, skip_ref, s_ref, run_ref, runt_ref,
    b_ref, c_ref, sc_ref, bs_ref, bg_ref, sin_ref, gin_ref,
    out_ref, gx_ref, tail_ref, first_ref, tapg_ref, skipg_ref, dbc_ref, u_ref, v_ref, bnd_ref,
    xp, gp, zs, gs, bh, bl, ch, cl,
):
    p = pl.program_id(0)
    frames = x_ref.shape[0]
    blocks = frames // BLOCK
    square = (BLOCK, BLOCK)

    @pl.when(p == 0)
    def _():
        bh[...], bl[...] = split(b_ref[...])
        ch[...], cl[...] = split(c_ref[...])
        gs[...] = jnp.zeros_like(gs)
        dbc_ref[...] = jnp.zeros_like(dbc_ref)
        u_ref[...] = jnp.zeros_like(u_ref)
        v_ref[...] = jnp.zeros_like(v_ref)
        bnd_ref[...] = jnp.zeros_like(bnd_ref)

    pre = conv_x_pre(xp, halo_ref, x_ref, taps_ref)
    gate = 1.0 / (1.0 + jnp.exp(-pre))
    xa = pre * gate
    slope = gate * (1.0 + pre * (1.0 - gate))
    back = lax.rem(LANES - 2 * p, LANES)
    causal = row_ids(square) >= lane_ids(square)
    low = lane_ids(square) < P_SIZE
    heads = jnp.where(
        lane_ids(square) == 2 * p + row_ids(square) // P_SIZE, 1.0, 0.0
    ).astype(BF16)
    nothing = jnp.zeros(square, BF16)

    runs = []
    decays = []
    for k in range(blocks):
        rolled = pltpu.roll(run_ref[rows_of(k), :], back, 1)
        runs.append(rolled)
        wide = pair_columns(rolled[BLOCK - 8 : BLOCK, :])
        decays.append(jnp.exp(wide[7:8, :]))
    grads = [None] * blocks
    grad = gin_ref[0]
    for k in reversed(range(blocks)):
        grads[k] = grad
        grad = decays[k] * grad + bg_ref[0, k]

    state = sin_ref[0]
    for k in range(blocks):
        rows = rows_of(k)
        x = xa[rows, :]
        gyh = gy_ref[rows, :]
        gy = gyh.astype(F32)
        run = pair_columns(runs[k])
        step = pair_columns(pltpu.roll(s_ref[rows, :], back, 1))
        reach = jnp.exp(run)
        to_end = jnp.exp(run[BLOCK - 1 : BLOCK, :] - run)
        xs = x * step
        xsh, xsl = split(xs)
        stored = split(state)
        graded = split(grads[k])
        b2 = (bh[rows, :], bl[rows, :])
        c2 = (ch[rows, :], cl[rows, :])
        gy_heads = jnp.concatenate(
            [jnp.where(low, gyh, nothing), jnp.where(low, nothing, gyh)], axis=0
        )
        prod = mm(gy_heads, xsh, NT) + mm(gy_heads, xsl, NT)
        weights = []
        score_grad = gs[k]
        for half in range(2):
            gap = runs[k][:, half : half + 1] - runt_ref[k, pl.ds(2 * p + half, 1), :]
            decay = jnp.exp(jnp.where(causal, gap, -jnp.inf))
            weights.append(split(sc_ref[k] * decay))
            score_grad = score_grad + decay * prod[half * BLOCK : (half + 1) * BLOCK, :]
        gs[k] = score_grad
        wh = jnp.concatenate([weights[0][0], weights[1][0]], axis=1)
        wl = jnp.concatenate([weights[0][1], weights[1][1]], axis=1)
        xh2 = jnp.concatenate(
            [jnp.where(low, xsh, nothing), jnp.where(low, nothing, xsh)], axis=0
        )
        xl2 = jnp.concatenate(
            [jnp.where(low, xsl, nothing), jnp.where(low, nothing, xsl)], axis=0
        )
        y_scan = mm(wh, xh2) + (mm(wh, xl2) + mm(wl, xh2)) + reach * dot3(c2, stored)
        tall_h = jnp.concatenate([weights[0][0], weights[1][0]], axis=0)
        tall_l = jnp.concatenate([weights[0][1], weights[1][1]], axis=0)
        z = mm(tall_h, gy_heads, TN) + mm(tall_l, gy_heads, TN) + to_end * dot3(b2, graded)
        out_ref[rows, :] = (y_scan + skip_ref[0:1, :] * x).astype(BF16)
        zs[rows, :] = z * step + skip_ref[0:1, :] * gy
        u2 = split(gy * y_scan)
        v2 = split(x * z)
        u_ref[rows, :] += mm(u2[0], heads) + mm(u2[1], heads)
        v_ref[rows, :] += mm(v2[0], heads) + mm(v2[1], heads)
        dbc_ref[rows, :N] += dot3(split(xs * to_end), graded, NT)
        dbc_ref[rows, N:] += dot3(split(gy * reach), stored, NT)
        state = decays[k] * state + bs_ref[0, k]
        crossing = jnp.broadcast_to(jnp.sum(state * grads[k], axis=0, keepdims=True), (8, LANES))
        cross2 = split(crossing)
        bnd_ref[k] += mm(cross2[0], heads) + mm(cross2[1], heads)

    skipg_ref[...] = jnp.broadcast_to(
        jnp.sum(xa * gy_ref[...].astype(F32), axis=0, keepdims=True), (8, LANES)
    )
    g = zs[...] * slope
    gp[0:frames, :] = g
    gp[frames : frames + 8, :] = jnp.zeros((8, LANES), F32)
    gx = taps_ref[0:1, :] * gp[3 : 3 + frames, :]
    for k in range(1, 4):
        gx = gx + taps_ref[k : k + 1, :] * gp[3 - k : 3 - k + frames, :]
    gx_ref[...] = gx.astype(BF16)
    tail_ref[...] = gx[frames - 8 :, :]
    first_ref[...] = g[0:8, :]
    for k in range(4):
        tapg_ref[k : k + 1, :] = jnp.sum(
            g * xp[5 + k : 5 + k + frames, :], axis=0, keepdims=True
        )

    @pl.when(p == pl.num_programs(0) - 1)
    def _():
        for k in range(blocks):
            rows = rows_of(k)
            gk = split(gs[k])
            gt = split(gs[k].T)
            dbc_ref[rows, :N] += dot3(gt, (ch[rows, :], cl[rows, :]))
            dbc_ref[rows, N:] += dot3(gk, (bh[rows, :], bl[rows, :]))


def local(x_raw, bc_raw, dt_raw, conv_x, conv_bc, dt_bias, a_log, skip_d, d_out):
    margin = conv_x.shape[0] - 1
    frames, width = x_raw.shape
    head_count = dt_raw.shape[1]
    blocks = frames // BLOCK
    pairs = width // LANES
    size = lax.axis_size("seq")
    shape = jax.ShapeDtypeStruct

    tails = jnp.concatenate([x_raw[-margin:], bc_raw[-margin:]], axis=1)
    before = shifted(tails, "seq", 1)
    halo = jnp.pad(before.astype(F32), ((8 - margin, 0), (0, 0)))
    x_halo = halo[:, :width]
    bc_ext = jnp.concatenate([halo[:, width:], bc_raw.astype(F32)], axis=0)
    raw_sum = dt_raw + dt_bias
    step_size = jax.nn.softplus(raw_sum)
    rates = jnp.exp(a_log)
    log_decay = -step_size * rates
    padding = ((0, 0), (0, LANES - head_count))
    s_pad = jnp.pad(step_size, padding)
    la_pad = jnp.pad(log_decay, padding)
    skip_wide = jnp.broadcast_to(jnp.repeat(skip_d, P_SIZE)[None], (8, width))

    def whole(*dims):
        return pl.BlockSpec(dims, lambda p: (0,) * len(dims))

    def columns(rows):
        return pl.BlockSpec((rows, LANES), lambda p: (0, p))

    def pair(*dims):
        return pl.BlockSpec((1,) + dims, lambda p: (p,) + (0,) * len(dims))

    bs, bg, ls, lg, dec, run, b_act, c_act, scores, runt = pl.pallas_call(
        terms_kernel,
        grid=(pairs,),
        in_specs=[
            columns(8), columns(frames), columns(frames), columns(4),
            whole(frames + 8, 2 * N), whole(4, 2 * N), whole(frames, LANES), whole(frames, LANES),
        ],
        out_specs=[
            pair(blocks, N, LANES), pair(blocks, N, LANES), pair(N, LANES), pair(N, LANES),
            pair(8, LANES), whole(frames, LANES), whole(frames, N), whole(frames, N),
            whole(blocks, BLOCK, BLOCK), whole(blocks, LANES, BLOCK),
        ],
        out_shape=[
            shape((pairs, blocks, N, LANES), F32), shape((pairs, blocks, N, LANES), F32),
            shape((pairs, N, LANES), F32), shape((pairs, N, LANES), F32),
            shape((pairs, 8, LANES), F32), shape((frames, LANES), F32),
            shape((frames, N), F32), shape((frames, N), F32),
            shape((blocks, BLOCK, BLOCK), F32), shape((blocks, LANES, BLOCK), F32),
        ],
        scratch_shapes=[pltpu.VMEM((frames + 8, LANES), F32)]
        + [pltpu.VMEM((blocks, N, BLOCK), BF16)] * 4,
        compiler_params=pltpu.CompilerParams(vmem_limit_bytes=VMEM_LIMIT),
        name="terms",
    )(x_halo, x_raw, d_out, conv_x, bc_ext, conv_bc, s_pad, la_pad)

    in_vmem = pl.BlockSpec(memory_space=pltpu.VMEM)
    state_in, grad_in = pl.pallas_call(
        lambda *refs: chain_kernel(size, *refs),
        in_specs=[in_vmem] * 3,
        out_specs=[in_vmem] * 2,
        out_shape=[shape((pairs, N, LANES), F32)] * 2,
        scratch_shapes=[pltpu.VMEM((pairs, N, LANES), F32)] * 4
        + [pltpu.SemaphoreType.DMA((pairs,))] * 4,
        compiler_params=pltpu.CompilerParams(
            collective_id=0, has_side_effects=True, vmem_limit_bytes=VMEM_LIMIT
        ),
        name="chain",
    )(ls, lg, dec)

    layer_out, grad_x, tail, first, tap_grad, skip_grad, bc_local, u, v, bnd = pl.pallas_call(
        main_kernel,
        grid=(pairs,),
        in_specs=[
            columns(8), columns(frames), columns(frames), columns(4), columns(8),
            whole(frames, LANES), whole(frames, LANES), whole(blocks, LANES, BLOCK),
            whole(frames, N), whole(frames, N), whole(blocks, BLOCK, BLOCK),
            pair(blocks, N, LANES), pair(blocks, N, LANES), pair(N, LANES), pair(N, LANES),
        ],
        out_specs=[
            columns(frames), columns(frames), columns(8), columns(8), columns(4), columns(8),
            whole(frames, 2 * N), whole(frames, LANES), whole(frames, LANES),
            whole(blocks, 8, LANES),
        ],
        out_shape=[
            shape((frames, width), BF16), shape((frames, width), BF16),
            shape((8, width), F32), shape((8, width), F32), shape((4, width), F32),
            shape((8, width), F32), shape((frames, 2 * N), F32),
            shape((frames, LANES), F32), shape((frames, LANES), F32),
            shape((blocks, 8, LANES), F32),
        ],
        scratch_shapes=[
            pltpu.VMEM((frames + 8, LANES), F32), pltpu.VMEM((frames + 8, LANES), F32),
            pltpu.VMEM((frames, LANES), F32), pltpu.VMEM((blocks, BLOCK, BLOCK), F32),
        ]
        + [pltpu.VMEM((frames, N), BF16)] * 4,
        compiler_params=pltpu.CompilerParams(vmem_limit_bytes=VMEM_LIMIT),
        name="main",
    )(
        x_halo, x_raw, d_out, conv_x, skip_wide, s_pad, run, runt,
        b_act, c_act, scores, bs, bg, state_in, grad_in,
    )

    bc_pre = conv_bc[0] * bc_ext[5 : 5 + frames]
    for k in range(1, 4):
        bc_pre = bc_pre + conv_bc[k] * bc_ext[5 + k : 5 + k + frames]
    gate = jax.nn.sigmoid(bc_pre)
    bc_grad = lax.psum(bc_local, "head") * (gate * (1.0 + bc_pre * (1.0 - gate)))
    conv_bc_grad = jnp.stack(
        [jnp.sum(bc_grad * bc_ext[5 + k : 5 + k + frames], axis=0) for k in range(4)]
    )
    after = shifted(jnp.concatenate([first[:margin], bc_grad[:margin]], axis=1), "seq", -1)
    bc_spread = jnp.concatenate([bc_grad, after[:, width:]], axis=0)
    grad_bc = conv_bc[0] * bc_spread[3 : 3 + frames]
    for k in range(1, 4):
        grad_bc = grad_bc + conv_bc[k] * bc_spread[3 - k : 3 - k + frames]
    x_after = jnp.pad(after[:, :width], ((margin, 0), (0, 0)))
    patch = tail[8 - margin :]
    for k in range(margin):
        patch = patch + conv_x[k] * x_after[3 - k : 6 - k]
    grad_x = lax.dynamic_update_slice(grad_x, patch.astype(BF16), (frames - margin, 0))

    u = u[:, :head_count]
    v = v[:, :head_count]
    net = (u - step_size * v).reshape(blocks, BLOCK, head_count)
    upper = (jnp.arange(BLOCK)[:, None] <= jnp.arange(BLOCK)[None, :]).astype(F32)
    g_log = jnp.einsum("tq,kqh->kth", upper, net, precision=lax.Precision.HIGHEST)
    g_log = (g_log + bnd[:, 0:1, :head_count]).reshape(frames, head_count)
    grad_steps = (v - g_log * rates) * jax.nn.sigmoid(raw_sum)
    skip_part = jnp.sum(skip_grad[0].reshape(head_count, P_SIZE), axis=1)
    summed = lax.psum(
        jnp.concatenate(
            [
                tap_grad.reshape(-1),
                conv_bc_grad.reshape(-1),
                jnp.sum(grad_steps, axis=0),
                jnp.sum(g_log * log_decay, axis=0),
                skip_part,
            ]
        ),
        "seq",
    )
    cuts = [4 * width, 8 * N, head_count, head_count, head_count]
    parts = []
    at = 0
    for cut in cuts:
        parts.append(summed[at : at + cut])
        at += cut
    return (
        layer_out,
        grad_x,
        grad_bc,
        grad_steps,
        parts[0].reshape(4, width),
        parts[1].reshape(4, 2 * N),
        parts[2],
        parts[3],
        parts[4],
    )


def solution(mesh):
    placed = (
        P("seq", "head"),
        P("seq", None),
        P("seq", "head"),
        P(None, "head"),
        P(),
        P("head"),
        P("head"),
        P("head"),
        P("seq", "head"),
    )
    return jax.shard_map(
        local,
        mesh=mesh,
        in_specs=placed,
        out_specs=(
            P("seq", "head"),
            P("seq", "head"),
            P("seq", None),
            P("seq", "head"),
            P(None, "head"),
            P(),
            P("head"),
            P("head"),
            P("head"),
        ),
        check_vma=False,
    )
```

time: 280 us -> 153 us (0.55)
  the two profiles are of different devices: /device:TPU:0 before, /device:TPU:27 now
where the time goes in v1:
time: 153 us; the launch traced here: 150 us
  Pallas kernels  51.4 us (34%)
  waiting for transfers between devices  39.8 us (26%)
  blocking collectives  22.3 us (15%)
  between operations  14.5 us (9%)
  local copies, waits for them, and re-layouts  10.4 us (7%)
  other arithmetic  5.93 us (4%)
  starting transfers between devices  5.77 us (4%)
    psum x1, waiting for transfers between devices, local(): lax.psum(bc_local, 'head') * (gate * (1.0 + bc_pre * (1.0 - gate)))  37 us
    psum x1, blocking collectives, local(): lax.psum(jnp.concatenate([tap_grad.reshape(-1), conv_bc_grad.reshape(-1),...  22.3 us
    pallas_call x1, Pallas kernels, local(): pl.pallas_call(main_kernel, grid=(pairs,), in_specs=[columns(8), columns(...  21.4 us
    pallas_call x1, Pallas kernels, local(): pl.pallas_call(lambda *refs: chain_kernel(size, *refs), in_specs=[in_vmem...  19.9 us
    pallas_call x1, Pallas kernels, local(): pl.pallas_call(terms_kernel, grid=(pairs,), in_specs=[columns(8), columns...  10.2 us
    ppermute x2, starting transfers between devices, shifted(): return lax.ppermute(block, axis, route)  5.73 us
  transfers between devices with their start and end apart: 3, of which 2 were waited for; matrix products, arithmetic and copies ran while one was open for 7% of the time, Pallas kernels for 0%

profile of v1, /device:TPU:27, one launch (start us, length us, event | category | flops | bytes accessed | tf_op | source)
XLA Modules:
  0.0 150.4 jit_solution(784466903868142474)
XLA Ops:
  7.2 0.7 slice.107
  8.0 0.7 slice.108
  8.7 3.8 %collective-permute-start = (bf16[3,1280]{1,0:T(4,128)(2,1)S(1)}, bf16[3,1280]{1,0:T(4,128)(2,1)S(1)}, u32[]{:S(2)}, u32[]{:S(2)}) collective-permute-start(bf16[3,1280]{1,0:T(4,128)(2,1)S(1)} %pad_maximum_fusion.3), channel_id=1, source_target_pairs={{0,4},{4,8},{8,12},{12,16},{16,20},{20,24},{24,28},{1,5},{5,9},{9,... | collective-permute-start | bytes 23048 | tf_op jit(solution)/shard_map/ppermute | solution.py:24
  12.5 0.9 copy.18
  13.4 0.7 exp.14
  14.1 1.4 fusion.25
  15.5 0.8 negate_multiply_fusion
  16.4 1.5 fusion.26
  17.9 1.0 convert_element_type.15
  19.2 10.2 %terms.1 = (f32[8,4,128,128]{3,2,1,0:T(8,128)S(1)}, f32[8,4,128,128]{3,2,1,0:T(8,128)S(1)}, f32[8,128,128]{2,1,0:T(8,128)S(1)}, f32[8,128,128]{2,1,0:T(8,128)S(1...) custom-call(f32[8,1024]{1,0:T(8,128)S(1)} %slice.140.halo_ref, ...), custom_call_target="tpu_custom_call" | custom-call | tf_op jit(solution)/shard_map/terms/pallas_call | solution.py:387
  29.4 19.9 %chain.1 = (f32[8,128,128]{2,1,0:T(8,128)S(1)}, f32[8,128,128]{2,1,0:T(8,128)S(1)}) custom-call(f32[8,128,128]{2,1,0:T(8,128)S(1)} %get-tuple-element.38.refs_0_, f32[8,128,128]{2,1,0:T(8,128)S(1)} %get-tuple-element.39.refs_1_, f32[8,8,128]{2,1,0:T(8,128)S(1)} %get-tuple-element.40.refs_2_), custom_call_target="tpu_custom_call" | custom-call | tf_op jit(solution)/shard_map/chain/pallas_call | solution.py:413
  49.3 21.4 %main.1 = (bf16[512,1024]{1,0:T(8,128)(2,1)}, bf16[512,1024]{1,0:T(8,128)(2,1)}, f32[8,1024]{1,0:T(8,128)S(1)}, f32[8,1024]{1,0:T(8,128)S(1)}, f32[4,1024]{1,0:T...) custom-call(f32[8,1024]{1,0:T(8,128)S(1)} %slice.140.halo_ref, ...), custom_call_target="tpu_custom_call" | custom-call | tf_op jit(solution)/shard_map/main/pallas_call | solution.py:426
  70.8 1.1 multiply_subtract_fusion
  72.8 0.7 copy.21
  73.6 37.0 %all-reduce.6.cloned.1.call-done = f32[512,256]{1,0:T(8,128)} async-done(((f32[512,256]{1,0:T(8,128)}), f32[512,256]{1,0:T(8,128)}) %all-reduce.6.cloned.1.call-update) | async-done | bytes 524304 | tf_op jit(solution)/shard_map/psum | solution.py:463
  110.6 1.6 %multiply_reduce_fusion.3 = (f32[256]{0:T(256)S(1)}, f32[256]{0:T(256)S(1)}, f32[256]{0:T(256)S(1)}, f32[256]{0:T(256)S(1)}, f32[512,256]{1,0:T(8,128)S(1)}) fusion(f32[512,256]{1,0:T(8,128)S(1)} %convert_element_type.15, f32[8,256]{1,0:T(8,128)S(1)} %copy-done.11, bf16[512,256]{1,0:T(8,128)(2,1)S(1)} %copy-done.9, ...), kind=kLoop, calls=%fused_computation.24 | loop fusion | flops 3931136 | bytes 1851392 | tf_op jit(solution)/shard_map/reduce_sum | solution.py:465
  112.3 22.3 %psum.15 = f32[5168]{0:T(1024)S(1)} all-reduce(f32[5168]{0:T(1024)S(1)} %concatenate.19), channel_id=1, replica_groups=mesh['seq'=8,'head'=4] {'seq'}, use_global_device_ids=true, to_apply=%region_8.9 | all-reduce | flops 5168 | bytes 41344 | tf_op jit(solution)/shard_map/psum | solution.py:486
  134.6 1.9 %collective-permute-start.1 = (f32[3,1280]{1,0:T(4,128)S(1)}, f32[3,1280]{1,0:T(4,128)S(1)}, u32[]{:S(2)}, u32[]{:S(2)}) collective-permute-start(f32[3,1280]{1,0:T(4,128)S(1)} %pad_maximum_fusion.2), channel_id=1, source_target_pairs={{4,0},{8,4},{12,8},{16,12},{20,16},{24,20},{28,24},{5,1},{9,5},{13... | collective-permute-start | bytes 46088 | tf_op jit(solution)/shard_map/ppermute | solution.py:24
  136.6 0.6 fusion.24
  137.1 0.6 reshape.43
  137.8 0.6 reshape.44
  138.4 2.8 %collective-permute-done.1 = f32[3,1280]{1,0:T(4,128)S(1)} collective-permute-done((f32[3,1280]{1,0:T(4,128)S(1)}, f32[3,1280]{1,0:T(4,128)S(1)}, u32[]{:S(2)}, u32[]{:S(2)}) %collective-permute-start.1) | collective-permute-done | bytes 15392 | tf_op jit(solution)/shard_map/ppermute | solution.py:24
  141.2 1.0 fusion.5
  142.2 1.4 dynamic_update_slice.3
  (78 shorter events, 1.4 us)
Async XLA Ops:
  7.2 11.8 %copy-start.22 = (f32[16]{0:T(128)S(1)}, f32[16]{0:T(128)}, u32[]{:S(2)}) copy-start(f32[16]{0:T(128)} %param.16) | copy-start | bytes 196
  7.2 103.4 %all-reduce.6.cloned.1.call-start = ((), (), s32[]{:S(2)}) async-start(), calls=%async_computation | async-start | bytes 1048576 | tf_op jit(solution)/shard_map/psum | solution.py:463
  8.7 10.6 %copy-start = (bf16[512,1024]{1,0:T(8,128)(2,1)S(1)}, bf16[512,1024]{1,0:T(8,128)(2,1)}, u32[]{:S(2)}) copy-start(bf16[512,1024]{1,0:T(8,128)(2,1)} %x_ref.3) | copy-start | bytes 3145732
  8.7 10.6 %copy-start.1 = (bf16[512,1024]{1,0:T(8,128)(2,1)S(1)}, bf16[512,1024]{1,0:T(8,128)(2,1)}, u32[]{:S(2)}) copy-start(bf16[512,1024]{1,0:T(8,128)(2,1)} %gy_ref.3) | copy-start | bytes 3145732
  8.7 10.6 %copy-start.2 = (f32[4,1024]{1,0:T(4,128)S(1)}, f32[4,1024]{1,0:T(4,128)}, u32[]{:S(2)}) copy-start(f32[4,1024]{1,0:T(4,128)} %taps_ref.3) | copy-start | bytes 49156
  8.7 10.6 %copy-start.3 = (f32[4,256]{1,0:T(4,128)S(1)}, f32[4,256]{1,0:T(4,128)}, u32[]{:S(2)}) copy-start(f32[4,256]{1,0:T(4,128)} %taps_bc_ref.1) | copy-start | bytes 12292
  8.7 10.4 %collective-permute-start = (bf16[3,1280]{1,0:T(4,128)(2,1)S(1)}, bf16[3,1280]{1,0:T(4,128)(2,1)S(1)}, u32[]{:S(2)}, u32[]{:S(2)}) collective-permute-start(bf16[3,1280]{1,0:T(4,128)(2,1)S(1)} %pad_maximum_fusion.3), channel_id=1, source_target_pairs={{0,4},{4,8},{8,12},{12,16},{16,20},{20,24},{24,28},{1,5},{5,9},{9,... | collective-permute-start | bytes 23048 | tf_op jit(solution)/shard_map/ppermute | solution.py:24
  13.4 5.5 %copy-start.4 = (f32[512,16]{1,0:T(8,128)}, f32[512,16]{1,0:T(8,128)S(1)}, u32[]{:S(2)}) copy-start(f32[512,16]{1,0:T(8,128)S(1)} %copy.18) | copy-start | bytes 98308
  14.1 4.8 %copy-start.20 = (f32[16]{0:T(128)}, f32[16]{0:T(128)S(1)}, u32[]{:S(2)}) copy-start(f32[16]{0:T(128)S(1)} %exp.14) | copy-start | bytes 196
  16.4 2.5 %copy-start.6 = (f32[512,16]{1,0:T(8,128)}, f32[512,16]{1,0:T(8,128)S(1)}, u32[]{:S(2)}) copy-start(f32[512,16]{1,0:T(8,128)S(1)} %get-tuple-element.69) | copy-start | bytes 98308
  16.4 2.6 %copy-start.8 = (f32[512,16]{1,0:T(8,128)}, f32[512,16]{1,0:T(8,128)S(1)}, u32[]{:S(2)}) copy-start(f32[512,16]{1,0:T(8,128)S(1)} %get-tuple-element.70) | copy-start | bytes 98308
  19.2 10.3 %copy-start.10 = (f32[8,256]{1,0:T(8,128)}, f32[8,256]{1,0:T(8,128)S(1)}, u32[]{:S(2)}) copy-start(f32[8,256]{1,0:T(8,128)S(1)} %pad_convert_fusion.1) | copy-start | bytes 24580
  70.7 2.0 %copy-start.5 = (f32[512,16]{1,0:T(8,128)S(1)}, f32[512,16]{1,0:T(8,128)}, u32[]{:S(2)}) copy-start(f32[512,16]{1,0:T(8,128)} %copy-done.4) | copy-start | bytes 98308
  70.7 1.9 %copy-start.7 = (f32[512,16]{1,0:T(8,128)S(1)}, f32[512,16]{1,0:T(8,128)}, u32[]{:S(2)}) copy-start(f32[512,16]{1,0:T(8,128)} %copy-done.6) | copy-start | bytes 98308
  70.7 39.8 %copy-start.9 = (bf16[512,256]{1,0:T(8,128)(2,1)S(1)}, bf16[512,256]{1,0:T(8,128)(2,1)}, u32[]{:S(2)}) copy-start(bf16[512,256]{1,0:T(8,128)(2,1)} %param.10) | copy-start | bytes 786436
  70.7 39.8 %copy-start.11 = (f32[8,256]{1,0:T(8,128)S(1)}, f32[8,256]{1,0:T(8,128)}, u32[]{:S(2)}) copy-start(f32[8,256]{1,0:T(8,128)} %copy-done.10) | copy-start | bytes 24580
  70.7 39.8 %copy-start.15 = (f32[1,256]{1,0:T(1,128)S(1)}, f32[1,256]{1,0:T(1,128)}, u32[]{:S(2)}) copy-start(f32[1,256]{1,0:T(1,128)} %get-tuple-element.78) | copy-start | bytes 3076
  70.8 39.8 %copy-start.16 = (f32[1,256]{1,0:T(1,128)S(1)}, f32[1,256]{1,0:T(1,128)}, u32[]{:S(2)}) copy-start(f32[1,256]{1,0:T(1,128)} %get-tuple-element.79) | copy-start | bytes 3076
  70.8 39.8 %copy-start.17 = (f32[1,256]{1,0:T(1,128)S(1)}, f32[1,256]{1,0:T(1,128)}, u32[]{:S(2)}) copy-start(f32[1,256]{1,0:T(1,128)} %get-tuple-element.80) | copy-start | bytes 3076
  70.8 39.8 %copy-start.18 = (f32[1,256]{1,0:T(1,128)S(1)}, f32[1,256]{1,0:T(1,128)}, u32[]{:S(2)}) copy-start(f32[1,256]{1,0:T(1,128)} %get-tuple-element.81) | copy-start | bytes 3076
  72.8 69.4 %copy-start.12 = (f32[1,1024]{1,0:T(1,128)S(1)}, f32[1,1024]{1,0:T(1,128)}, u32[]{:S(2)}) copy-start(f32[1,1024]{1,0:T(1,128)} %get-tuple-element.75) | copy-start | bytes 12292
  72.8 69.4 %copy-start.13 = (f32[1,1024]{1,0:T(1,128)S(1)}, f32[1,1024]{1,0:T(1,128)}, u32[]{:S(2)}) copy-start(f32[1,1024]{1,0:T(1,128)} %get-tuple-element.76) | copy-start | bytes 12292
  72.8 69.4 %copy-start.14 = (f32[1,1024]{1,0:T(1,128)S(1)}, f32[1,1024]{1,0:T(1,128)}, u32[]{:S(2)}) copy-start(f32[1,1024]{1,0:T(1,128)} %get-tuple-element.77) | copy-start | bytes 12292
  134.6 6.5 %collective-permute-start.1 = (f32[3,1280]{1,0:T(4,128)S(1)}, f32[3,1280]{1,0:T(4,128)S(1)}, u32[]{:S(2)}, u32[]{:S(2)}) collective-permute-start(f32[3,1280]{1,0:T(4,128)S(1)} %pad_maximum_fusion.2), channel_id=1, source_target_pairs={{4,0},{8,4},{12,8},{16,12},{20,16},{24,20},{28,24},{5,1},{9,5},{13... | collective-permute-start | bytes 46088 | tf_op jit(solution)/shard_map/ppermute | solution.py:24
  (2 other events, 3.9 us)
Sparse Core Ops, SparseCore 0:
  70.9 39.5 all-reduce.5

commit v2 on v1

--- a/solution.py
+++ b/solution.py
@@ -224,6 +224,92 @@
         return carry
 
     lax.fori_loop(0, chunks, drain, 0)
+
+
+def greet(axis, size, me):
+    barrier = pltpu.get_barrier_semaphore()
+    for d in range(1, size):
+        pl.semaphore_signal(
+            barrier, inc=1, device_id={axis: lax.rem(me + d, size)}, device_id_type=MESH
+        )
+    pl.semaphore_wait(barrier, size - 1)
+
+
+def share_kernel(size, in_ref, out_ref, got, send, recv):
+    me = lax.axis_index("seq")
+    greet("seq", size, me)
+
+    def copy(d, owner, target):
+        return pltpu.make_async_remote_copy(
+            src_ref=in_ref,
+            dst_ref=got.at[owner],
+            send_sem=send.at[d],
+            recv_sem=recv.at[owner],
+            device_id={"seq": target},
+            device_id_type=MESH,
+        )
+
+    for d in range(1, size):
+        copy(d, me, lax.rem(me + d, size)).start()
+    got[me] = in_ref[...]
+    for d in range(1, size):
+        source = lax.rem(me + size - d, size)
+        copy(d, source, source).wait_recv()
+    total = got[0]
+    for i in range(1, size):
+        total = total + got[i]
+    out_ref[...] = total
+    for d in range(1, size):
+        copy(d, me, lax.rem(me + d, size)).wait_send()
+
+
+def head_sum_kernel(size, in_ref, out_ref, got, send1, recv1, send2, recv2):
+    me = lax.axis_index("head")
+    greet("head", size, me)
+    rows = in_ref.shape[0] // size
+
+    def block(i):
+        return pl.ds(pl.multiple_of(i * rows, rows), rows)
+
+    def scatter(d, owner, target):
+        return pltpu.make_async_remote_copy(
+            src_ref=in_ref.at[block(target)],
+            dst_ref=got.at[owner],
+            send_sem=send1.at[d],
+            recv_sem=recv1.at[owner],
+            device_id={"head": target},
+            device_id_type=MESH,
+        )
+
+    def gather(d, owner, target):
+        return pltpu.make_async_remote_copy(
+            src_ref=out_ref.at[block(owner)],
+            dst_ref=out_ref.at[block(owner)],
+            send_sem=send2.at[d],
+            recv_sem=recv2.at[owner],
+            device_id={"head": target},
+            device_id_type=MESH,
+        )
+
+    for d in range(1, size):
+        scatter(d, me, lax.rem(me + d, size)).start()
+    got[me] = in_ref[block(me), :]
+    for d in range(1, size):
+        source = lax.rem(me + size - d, size)
+        scatter(d, source, source).wait_recv()
+    total = got[0]
+    for i in range(1, size):
+        total = total + got[i]
+    out_ref[block(me), :] = total
+    for d in range(1, size):
+        gather(d, me, lax.rem(me + d, size)).start()
+    for d in range(1, size):
+        source = lax.rem(me + size - d, size)
+        gather(d, source, source).wait_recv()
+    for d in range(1, size):
+        target = lax.rem(me + d, size)
+        scatter(d, me, target).wait_send()
+        gather(d, me, target).wait_send()
 
 
 def main_kernel(
@@ -456,11 +542,25 @@
         b_act, c_act, scores, bs, bg, state_in, grad_in,
     )
 
+    heads = lax.axis_size("head")
+    bc_total = pl.pallas_call(
+        lambda *refs: head_sum_kernel(heads, *refs),
+        in_specs=[in_vmem],
+        out_specs=in_vmem,
+        out_shape=shape((frames, 2 * N), F32),
+        scratch_shapes=[pltpu.VMEM((heads, frames // heads, 2 * N), F32)]
+        + [pltpu.SemaphoreType.DMA((heads,))] * 4,
+        compiler_params=pltpu.CompilerParams(
+            collective_id=1, has_side_effects=True, vmem_limit_bytes=VMEM_LIMIT
+        ),
+        name="head_sum",
+    )(bc_local)
+
     bc_pre = conv_bc[0] * bc_ext[5 : 5 + frames]
     for k in range(1, 4):
         bc_pre = bc_pre + conv_bc[k] * bc_ext[5 + k : 5 + k + frames]
     gate = jax.nn.sigmoid(bc_pre)
-    bc_grad = lax.psum(bc_local, "head") * (gate * (1.0 + bc_pre * (1.0 - gate)))
+    bc_grad = bc_total * (gate * (1.0 + bc_pre * (1.0 - gate)))
     conv_bc_grad = jnp.stack(
         [jnp.sum(bc_grad * bc_ext[5 + k : 5 + k + frames], axis=0) for k in range(4)]
     )
@@ -483,18 +583,29 @@
     g_log = (g_log + bnd[:, 0:1, :head_count]).reshape(frames, head_count)
     grad_steps = (v - g_log * rates) * jax.nn.sigmoid(raw_sum)
     skip_part = jnp.sum(skip_grad[0].reshape(head_count, P_SIZE), axis=1)
-    summed = lax.psum(
-        jnp.concatenate(
-            [
-                tap_grad.reshape(-1),
-                conv_bc_grad.reshape(-1),
-                jnp.sum(grad_steps, axis=0),
-                jnp.sum(g_log * log_decay, axis=0),
-                skip_part,
-            ]
+    flat = jnp.concatenate(
+        [
+            tap_grad.reshape(-1),
+            conv_bc_grad.reshape(-1),
+            jnp.sum(grad_steps, axis=0),
+            jnp.sum(g_log * log_decay, axis=0),
+            skip_part,
+        ]
+    )
+    lines = -(-flat.shape[0] // (8 * LANES)) * 8
+    flat = jnp.pad(flat, (0, lines * LANES - flat.shape[0])).reshape(lines, LANES)
+    summed = pl.pallas_call(
+        lambda *refs: share_kernel(size, *refs),
+        in_specs=[in_vmem],
+        out_specs=in_vmem,
+        out_shape=shape((lines, LANES), F32),
+        scratch_shapes=[pltpu.VMEM((size, lines, LANES), F32)]
+        + [pltpu.SemaphoreType.DMA((size,))] * 2,
+        compiler_params=pltpu.CompilerParams(
+            collective_id=2, has_side_effects=True, vmem_limit_bytes=VMEM_LIMIT
         ),
-        "seq",
-    )
+        name="share",
+    )(flat).reshape(-1)
     cuts = [4 * width, 8 * N, head_count, head_count, head_count]
     parts = []
     at = 0

time: 153 us -> 111 us (0.73); the launches traced: 150 us -> 111 us
  waiting for transfers between devices: 39.8 us -> 1.14 us
  Pallas kernels: 51.4 us -> 88.3 us
  blocking collectives: 22.3 us -> 0 us
  between operations: 14.5 us -> 1.08 us
  other arithmetic: 5.93 us -> 3.84 us
    pallas_call x0 -> x2, Pallas kernels: none -> 37 us  [the longest x1 28.5 us: local(): pl.pallas_call(lambda *refs: head_sum_kernel(heads, *refs), in_specs=[in_...]
    psum x1 -> x0, waiting for transfers between devices: 37 us -> none  [local(): lax.psum(bc_local, 'head') * (gate * (1.0 + bc_pre * (1.0 - gate)))]
    psum x1 -> x0, blocking collectives: 22.3 us -> none  [local(): lax.psum(jnp.concatenate([tap_grad.reshape(-1), conv_bc_grad.reshape(-1),...]
    ppermute x2, waiting for transfers between devices: 2.8 us -> 1.14 us  [shifted(): return lax.ppermute(block, axis, route)]
  transfers between devices with their start and end apart: 3 -> 2, of which waited for: 2 -> 1; matrix products, arithmetic and copies ran while one was open for 7% -> 8% of each run, Pallas kernels for 0% -> 0%
where the time goes in v2:
time: 111 us
  Pallas kernels  88.3 us (80%)
  local copies, waits for them, and re-layouts  9.8 us (9%)
  starting transfers between devices  6.14 us (6%)
  other arithmetic  3.84 us (3%)
  waiting for transfers between devices  1.14 us (1%)
    pallas_call x1, Pallas kernels, local(): pl.pallas_call(lambda *refs: head_sum_kernel(heads, *refs), in_specs=[in_...  28.5 us
    pallas_call x1, Pallas kernels, local(): pl.pallas_call(main_kernel, grid=(pairs,), in_specs=[columns(8), columns(...  21.3 us
    pallas_call x1, Pallas kernels, local(): pl.pallas_call(lambda *refs: chain_kernel(size, *refs), in_specs=[in_vmem...  19.9 us
    pallas_call x1, Pallas kernels, local(): pl.pallas_call(terms_kernel, grid=(pairs,), in_specs=[columns(8), columns...  10.2 us
    pallas_call x1, Pallas kernels, local(): pl.pallas_call(lambda *refs: share_kernel(size, *refs), in_specs=[in_vmem...  8.54 us
    ppermute x2, starting transfers between devices, shifted(): return lax.ppermute(block, axis, route)  6.14 us
  transfers between devices with their start and end apart: 2, of which 1 were waited for; matrix products, arithmetic and copies ran while one was open for 8% of the time, Pallas kernels for 0%

profile of v2, /device:TPU:27, one launch (start us, length us, event | category | flops | bytes accessed | tf_op | source)
XLA Modules:
  0.0 110.7 jit_solution(16576693114638477824)
XLA Ops:
  0.7 0.7 slice.109
  1.4 0.7 slice.110
  2.1 3.8 %collective-permute-start = (bf16[3,1280]{1,0:T(4,128)(2,1)S(1)}, bf16[3,1280]{1,0:T(4,128)(2,1)S(1)}, u32[]{:S(2)}, u32[]{:S(2)}) collective-permute-start(bf16[3,1280]{1,0:T(4,128)(2,1)S(1)} %pad_maximum_fusion.3), channel_id=1, source_target_pairs={{0,4},{4,8},{8,12},{12,16},{16,20},{20,24},{24,28},{1,5},{5,9},{9,... | collective-permute-start | bytes 23048 | tf_op jit(solution)/shard_map/ppermute | solution.py:24
  5.9 0.9 copy.18
  6.8 0.7 exp.14
  7.5 0.8 fusion.25
  8.3 0.8 negate_multiply_fusion
  9.2 1.5 %fusion.26 = (f32[1,256]{1,0:T(1,128)S(1)}, f32[1,256]{1,0:T(1,128)}, f32[1,256]{1,0:T(1,128)}, f32[1,256]{1,0:T(1,128)}) fusion(f32[4,256]{1,0:T(4,128)} %taps_bc_ref.1), kind=kLoop, calls=%fused_computation.53 | loop fusion | bytes 8192 | tf_op jit(solution)/shard_map/slice | solution.py:559
  10.7 1.0 convert_element_type.17
  12.0 10.2 %terms.1 = (f32[8,4,128,128]{3,2,1,0:T(8,128)S(1)}, f32[8,4,128,128]{3,2,1,0:T(8,128)S(1)}, f32[8,128,128]{2,1,0:T(8,128)S(1)}, f32[8,128,128]{2,1,0:T(8,128)S(1...) custom-call(f32[8,1024]{1,0:T(8,128)S(1)} %slice.142.halo_ref, ...), custom_call_target="tpu_custom_call" | custom-call | tf_op jit(solution)/shard_map/terms/pallas_call | solution.py:473
  22.2 19.9 %chain.1 = (f32[8,128,128]{2,1,0:T(8,128)S(1)}, f32[8,128,128]{2,1,0:T(8,128)S(1)}) custom-call(f32[8,128,128]{2,1,0:T(8,128)S(1)} %get-tuple-element.38.refs_0_, f32[8,128,128]{2,1,0:T(8,128)S(1)} %get-tuple-element.39.refs_1_, f32[8,8,128]{2,1,0:T(8,128)S(1)} %get-tuple-element.40.refs_2_), custom_call_target="tpu_custom_call" | custom-call | tf_op jit(solution)/shard_map/chain/pallas_call | solution.py:499
  42.2 21.3 %main.1 = (bf16[512,1024]{1,0:T(8,128)(2,1)}, bf16[512,1024]{1,0:T(8,128)(2,1)}, f32[8,1024]{1,0:T(8,128)S(1)}, f32[8,1024]{1,0:T(8,128)S(1)}, f32[4,1024]{1,0:T...) custom-call(f32[8,1024]{1,0:T(8,128)S(1)} %slice.142.halo_ref, ...), custom_call_target="tpu_custom_call" | custom-call | tf_op jit(solution)/shard_map/main/pallas_call | solution.py:512
  63.4 28.5 %head_sum.1 = f32[512,256]{1,0:T(8,128)S(1)} custom-call(f32[512,256]{1,0:T(8,128)S(1)} %get-tuple-element.47.refs_0_), custom_call_target="tpu_custom_call" | custom-call | tf_op jit(solution)/shard_map/head_sum/pallas_call | solution.py:546
  92.0 0.6 multiply_reduce_fusion.3
  92.7 0.3 fusion
  93.7 8.5 %share.1 = f32[48,128]{1,0:T(8,128)S(1)} custom-call(f32[48,128]{1,0:T(8,128)S(1)} %pad_bitcast_fusion.refs_0_), custom_call_target="tpu_custom_call" | custom-call | tf_op jit(solution)/shard_map/share/pallas_call | solution.py:597
  102.2 2.3 %collective-permute-start.1 = (f32[3,1280]{1,0:T(4,128)S(1)}, f32[3,1280]{1,0:T(4,128)S(1)}, u32[]{:S(2)}, u32[]{:S(2)}) collective-permute-start(f32[3,1280]{1,0:T(4,128)S(1)} %pad_maximum_fusion.2), channel_id=1, source_target_pairs={{4,0},{8,4},{12,8},{16,12},{20,16},{24,20},{28,24},{5,1},{9,5},{13... | collective-permute-start | bytes 46088 | tf_op jit(solution)/shard_map/ppermute | solution.py:24
  104.6 0.6 fusion.24
  105.2 0.6 reshape.54
  105.8 0.6 reshape.55
  106.4 0.7 copy.21
  107.1 1.1 %collective-permute-done.1 = f32[3,1280]{1,0:T(4,128)S(1)} collective-permute-done((f32[3,1280]{1,0:T(4,128)S(1)}, f32[3,1280]{1,0:T(4,128)S(1)}, u32[]{:S(2)}, u32[]{:S(2)}) %collective-permute-start.1) | collective-permute-done | bytes 15392 | tf_op jit(solution)/shard_map/ppermute | solution.py:24
  108.3 1.0 fusion.5
  109.3 1.4 %dynamic_update_slice.3 = bf16[512,1024]{1,0:T(8,128)(2,1)} dynamic-update-slice(bf16[512,1024]{1,0:T(8,128)(2,1)} %get-tuple-element.44, bf16[3,1024]{1,0:T(4,128)(2,1)S(1)} %fusion.20, s32[]{:T(128)} %constant.12.clone.1, s32[]{:T(128)} %constant.13.clone.1) | dynamic-update-slice | bytes 12292 | tf_op jit(solution)/shard_map/dynamic_update_slice | solution.py:576
  (69 shorter events, 1.0 us)
Async XLA Ops:
  0.6 11.1 %copy-start.18 = (f32[16]{0:T(128)S(1)}, f32[16]{0:T(128)}, u32[]{:S(2)}) copy-start(f32[16]{0:T(128)} %param.16) | copy-start | bytes 196
  2.1 9.9 %copy-start = (bf16[512,1024]{1,0:T(8,128)(2,1)S(1)}, bf16[512,1024]{1,0:T(8,128)(2,1)}, u32[]{:S(2)}) copy-start(bf16[512,1024]{1,0:T(8,128)(2,1)} %x_ref.3) | copy-start | bytes 3145732
  2.1 9.9 %copy-start.1 = (bf16[512,1024]{1,0:T(8,128)(2,1)S(1)}, bf16[512,1024]{1,0:T(8,128)(2,1)}, u32[]{:S(2)}) copy-start(bf16[512,1024]{1,0:T(8,128)(2,1)} %gy_ref.3) | copy-start | bytes 3145732
  2.1 9.9 %copy-start.2 = (f32[4,1024]{1,0:T(4,128)S(1)}, f32[4,1024]{1,0:T(4,128)}, u32[]{:S(2)}) copy-start(f32[4,1024]{1,0:T(4,128)} %taps_ref.3) | copy-start | bytes 49156
  2.1 9.9 %copy-start.3 = (f32[4,256]{1,0:T(4,128)S(1)}, f32[4,256]{1,0:T(4,128)}, u32[]{:S(2)}) copy-start(f32[4,256]{1,0:T(4,128)} %taps_bc_ref.1) | copy-start | bytes 12292
  2.1 9.8 %collective-permute-start = (bf16[3,1280]{1,0:T(4,128)(2,1)S(1)}, bf16[3,1280]{1,0:T(4,128)(2,1)S(1)}, u32[]{:S(2)}, u32[]{:S(2)}) collective-permute-start(bf16[3,1280]{1,0:T(4,128)(2,1)S(1)} %pad_maximum_fusion.3), channel_id=1, source_target_pairs={{0,4},{4,8},{8,12},{12,16},{16,20},{20,24},{24,28},{1,5},{5,9},{9,... | collective-permute-start | bytes 23048 | tf_op jit(solution)/shard_map/ppermute | solution.py:24
  7.5 4.2 %copy-start.16 = (f32[16]{0:T(128)}, f32[16]{0:T(128)S(1)}, u32[]{:S(2)}) copy-start(f32[16]{0:T(128)S(1)} %exp.14) | copy-start | bytes 196
  9.2 2.5 %copy-start.6 = (f32[512,16]{1,0:T(8,128)}, f32[512,16]{1,0:T(8,128)S(1)}, u32[]{:S(2)}) copy-start(f32[512,16]{1,0:T(8,128)S(1)} %get-tuple-element.70) | copy-start | bytes 98308
  9.2 2.5 %copy-start.4 = (f32[512,16]{1,0:T(8,128)}, f32[512,16]{1,0:T(8,128)S(1)}, u32[]{:S(2)}) copy-start(f32[512,16]{1,0:T(8,128)S(1)} %get-tuple-element.69) | copy-start | bytes 98308
  42.1 49.8 %copy-start.8 = (bf16[512,256]{1,0:T(8,128)(2,1)S(1)}, bf16[512,256]{1,0:T(8,128)(2,1)}, u32[]{:S(2)}) copy-start(bf16[512,256]{1,0:T(8,128)(2,1)} %param.10) | copy-start | bytes 786436
  42.1 49.8 %copy-start.9 = (f32[1,256]{1,0:T(1,128)S(1)}, f32[1,256]{1,0:T(1,128)}, u32[]{:S(2)}) copy-start(f32[1,256]{1,0:T(1,128)} %get-tuple-element.79) | copy-start | bytes 3076
  42.1 49.8 %copy-start.11 = (f32[1,256]{1,0:T(1,128)S(1)}, f32[1,256]{1,0:T(1,128)}, u32[]{:S(2)}) copy-start(f32[1,256]{1,0:T(1,128)} %get-tuple-element.80) | copy-start | bytes 3076
  42.1 49.8 %copy-start.13 = (f32[1,256]{1,0:T(1,128)S(1)}, f32[1,256]{1,0:T(1,128)}, u32[]{:S(2)}) copy-start(f32[1,256]{1,0:T(1,128)} %get-tuple-element.81) | copy-start | bytes 3076
  63.4 29.2 %copy-start.7 = (f32[512,16]{1,0:T(8,128)S(1)}, f32[512,16]{1,0:T(8,128)}, u32[]{:S(2)}) copy-start(f32[512,16]{1,0:T(8,128)} %copy-done.6) | copy-start | bytes 98308
  63.4 29.8 %copy-start.5 = (f32[512,16]{1,0:T(8,128)S(1)}, f32[512,16]{1,0:T(8,128)}, u32[]{:S(2)}) copy-start(f32[512,16]{1,0:T(8,128)} %copy-done.4) | copy-start | bytes 98308
  63.4 29.8 %copy-start.15 = (f32[16]{0:T(128)S(1)}, f32[16]{0:T(128)}, u32[]{:S(2)}) copy-start(f32[16]{0:T(128)} %param.14) | copy-start | bytes 196
  63.4 29.8 %copy-start.17 = (f32[16]{0:T(128)S(1)}, f32[16]{0:T(128)}, u32[]{:S(2)}) copy-start(f32[16]{0:T(128)} %copy-done.16) | copy-start | bytes 196
  92.6 15.7 %copy-start.10 = (f32[1,256]{1,0:T(1,128)S(1)}, f32[1,256]{1,0:T(1,128)}, u32[]{:S(2)}) copy-start(f32[1,256]{1,0:T(1,128)} %get-tuple-element.79) | copy-start | bytes 3076
  92.6 15.7 %copy-start.12 = (f32[1,256]{1,0:T(1,128)S(1)}, f32[1,256]{1,0:T(1,128)}, u32[]{:S(2)}) copy-start(f32[1,256]{1,0:T(1,128)} %get-tuple-element.80) | copy-start | bytes 3076
  92.6 15.7 %copy-start.14 = (f32[1,256]{1,0:T(1,128)S(1)}, f32[1,256]{1,0:T(1,128)}, u32[]{:S(2)}) copy-start(f32[1,256]{1,0:T(1,128)} %get-tuple-element.81) | copy-start | bytes 3076
  102.2 6.0 %collective-permute-start.1 = (f32[3,1280]{1,0:T(4,128)S(1)}, f32[3,1280]{1,0:T(4,128)S(1)}, u32[]{:S(2)}, u32[]{:S(2)}) collective-permute-start(f32[3,1280]{1,0:T(4,128)S(1)} %pad_maximum_fusion.2), channel_id=1, source_target_pairs={{4,0},{8,4},{12,8},{16,12},{20,16},{24,20},{28,24},{5,1},{9,5},{13... | collective-permute-start | bytes 46088 | tf_op jit(solution)/shard_map/ppermute | solution.py:24

commit v3 on v2

--- a/solution.py
+++ b/solution.py
@@ -285,7 +285,7 @@
         return pltpu.make_async_remote_copy(
             src_ref=out_ref.at[block(owner)],
             dst_ref=out_ref.at[block(owner)],
-            send_sem=send2.at[d],
+            send_sem=send2.at[d, owner],
             recv_sem=recv2.at[owner],
             device_id={"head": target},
             device_id_type=MESH,
@@ -301,15 +301,38 @@
     for i in range(1, size):
         total = total + got[i]
     out_ref[block(me), :] = total
+    def relay(owner, way, start):
+        copy = gather(way, owner, me + 1 if way == 0 else me - 1)
+
+        @pl.when(me < size - 1 if way == 0 else me > 0)
+        def _():
+            copy.start() if start else copy.wait_send()
+
+    relay(me, 0, True)
+    relay(me, 1, True)
+    for k in range(1, size):
+        @pl.when(me - k >= 0)
+        def _():
+            gather(0, me - k, me).wait_recv()
+            relay(me - k, 0, True)
+
+        @pl.when(me + k < size)
+        def _():
+            gather(1, me + k, me).wait_recv()
+            relay(me + k, 1, True)
+
     for d in range(1, size):
-        gather(d, me, lax.rem(me + d, size)).start()
-    for d in range(1, size):
-        source = lax.rem(me + size - d, size)
-        gather(d, source, source).wait_recv()
-    for d in range(1, size):
-        target = lax.rem(me + d, size)
-        scatter(d, me, target).wait_send()
-        gather(d, me, target).wait_send()
+        scatter(d, me, lax.rem(me + d, size)).wait_send()
+    relay(me, 0, False)
+    relay(me, 1, False)
+    for k in range(1, size):
+        @pl.when(me - k >= 0)
+        def _():
+            relay(me - k, 0, False)
+
+        @pl.when(me + k < size)
+        def _():
+            relay(me + k, 1, False)
 
 
 def main_kernel(
@@ -549,7 +572,8 @@
         out_specs=in_vmem,
         out_shape=shape((frames, 2 * N), F32),
         scratch_shapes=[pltpu.VMEM((heads, frames // heads, 2 * N), F32)]
-        + [pltpu.SemaphoreType.DMA((heads,))] * 4,
+        + [pltpu.SemaphoreType.DMA((heads,))] * 2
+        + [pltpu.SemaphoreType.DMA((2, heads)), pltpu.SemaphoreType.DMA((heads,))],
         compiler_params=pltpu.CompilerParams(
             collective_id=1, has_side_effects=True, vmem_limit_bytes=VMEM_LIMIT
         ),

time: 111 us -> 113 us (1.018)
  the two profiles are of different devices: /device:TPU:27 before, /device:TPU:1 now
where the time goes in v3:
time: 113 us; the launch traced here: 112 us
  Pallas kernels  90.1 us (80%)
  local copies, waits for them, and re-layouts  9.8 us (9%)
  starting transfers between devices  6.71 us (6%)
  other arithmetic  3.84 us (3%)
    pallas_call x1, Pallas kernels, local(): pl.pallas_call(lambda *refs: head_sum_kernel(heads, *refs), in_specs=[in_...  26 us
    pallas_call x1, Pallas kernels, local(): pl.pallas_call(lambda *refs: chain_kernel(size, *refs), in_specs=[in_vmem...  24.2 us
    pallas_call x1, Pallas kernels, local(): pl.pallas_call(main_kernel, grid=(pairs,), in_specs=[columns(8), columns(...  21.3 us
    pallas_call x1, Pallas kernels, local(): pl.pallas_call(terms_kernel, grid=(pairs,), in_specs=[columns(8), columns...  10.2 us
    pallas_call x1, Pallas kernels, local(): pl.pallas_call(lambda *refs: share_kernel(size, *refs), in_specs=[in_vmem...  8.51 us
    ppermute x2, starting transfers between devices, shifted(): return lax.ppermute(block, axis, route)  6.71 us
  transfers between devices with their start and end apart: 2, of which 1 were waited for; matrix products, arithmetic and copies ran while one was open for 7% of the time, Pallas kernels for 0%

profile of v3, /device:TPU:1, one launch (start us, length us, event | category | flops | bytes accessed | tf_op | source)
XLA Modules:
  0.0 112.4 jit_solution(17040873068798635709)
XLA Ops:
  0.7 0.7 slice.109
  1.4 0.7 slice.110
  2.1 4.6 %collective-permute-start = (bf16[3,1280]{1,0:T(4,128)(2,1)S(1)}, bf16[3,1280]{1,0:T(4,128)(2,1)S(1)}, u32[]{:S(2)}, u32[]{:S(2)}) collective-permute-start(bf16[3,1280]{1,0:T(4,128)(2,1)S(1)} %pad_maximum_fusion.3), channel_id=1, source_target_pairs={{0,4},{4,8},{8,12},{12,16},{16,20},{20,24},{24,28},{1,5},{5,9},{9,... | collective-permute-start | bytes 23048 | tf_op jit(solution)/shard_map/ppermute | solution.py:24
  6.8 0.9 copy.18
  7.6 0.7 exp.14
  8.3 0.8 fusion.25
  9.2 0.8 negate_multiply_fusion
  10.0 1.5 %fusion.26 = (f32[1,256]{1,0:T(1,128)S(1)}, f32[1,256]{1,0:T(1,128)}, f32[1,256]{1,0:T(1,128)}, f32[1,256]{1,0:T(1,128)}) fusion(f32[4,256]{1,0:T(4,128)} %taps_bc_ref.1), kind=kLoop, calls=%fused_computation.53 | loop fusion | bytes 8192 | tf_op jit(solution)/shard_map/slice | solution.py:583
  11.5 1.0 convert_element_type.17
  12.9 10.2 %terms.1 = (f32[8,4,128,128]{3,2,1,0:T(8,128)S(1)}, f32[8,4,128,128]{3,2,1,0:T(8,128)S(1)}, f32[8,128,128]{2,1,0:T(8,128)S(1)}, f32[8,128,128]{2,1,0:T(8,128)S(1...) custom-call(f32[8,1024]{1,0:T(8,128)S(1)} %slice.142.halo_ref, ...), custom_call_target="tpu_custom_call" | custom-call | tf_op jit(solution)/shard_map/terms/pallas_call | solution.py:496
  23.1 24.2 %chain.1 = (f32[8,128,128]{2,1,0:T(8,128)S(1)}, f32[8,128,128]{2,1,0:T(8,128)S(1)}) custom-call(f32[8,128,128]{2,1,0:T(8,128)S(1)} %get-tuple-element.38.refs_0_, f32[8,128,128]{2,1,0:T(8,128)S(1)} %get-tuple-element.39.refs_1_, f32[8,8,128]{2,1,0:T(8,128)S(1)} %get-tuple-element.40.refs_2_), custom_call_target="tpu_custom_call" | custom-call | tf_op jit(solution)/shard_map/chain/pallas_call | solution.py:522
  47.3 21.3 %main.1 = (bf16[512,1024]{1,0:T(8,128)(2,1)}, bf16[512,1024]{1,0:T(8,128)(2,1)}, f32[8,1024]{1,0:T(8,128)S(1)}, f32[8,1024]{1,0:T(8,128)S(1)}, f32[4,1024]{1,0:T...) custom-call(f32[8,1024]{1,0:T(8,128)S(1)} %slice.142.halo_ref, ...), custom_call_target="tpu_custom_call" | custom-call | tf_op jit(solution)/shard_map/main/pallas_call | solution.py:535
  68.6 26.0 %head_sum.1 = f32[512,256]{1,0:T(8,128)S(1)} custom-call(f32[512,256]{1,0:T(8,128)S(1)} %get-tuple-element.47.refs_0_), custom_call_target="tpu_custom_call" | custom-call | tf_op jit(solution)/shard_map/head_sum/pallas_call | solution.py:569
  94.6 0.6 multiply_reduce_fusion.3
  95.3 0.3 fusion
  96.3 8.5 %share.1 = f32[48,128]{1,0:T(8,128)S(1)} custom-call(f32[48,128]{1,0:T(8,128)S(1)} %pad_bitcast_fusion.refs_0_), custom_call_target="tpu_custom_call" | custom-call | tf_op jit(solution)/shard_map/share/pallas_call | solution.py:621
  104.9 2.1 %collective-permute-start.1 = (f32[3,1280]{1,0:T(4,128)S(1)}, f32[3,1280]{1,0:T(4,128)S(1)}, u32[]{:S(2)}, u32[]{:S(2)}) collective-permute-start(f32[3,1280]{1,0:T(4,128)S(1)} %pad_maximum_fusion.2), channel_id=1, source_target_pairs={{4,0},{8,4},{12,8},{16,12},{20,16},{24,20},{28,24},{5,1},{9,5},{13... | collective-permute-start | bytes 46088 | tf_op jit(solution)/shard_map/ppermute | solution.py:24
  106.9 0.6 fusion.24
  107.5 0.6 reshape.54
  108.2 0.6 reshape.55
  108.8 0.7 copy.21
  109.5 0.5 collective-permute-done.1
  110.0 1.0 fusion.5
  111.0 1.4 %dynamic_update_slice.3 = bf16[512,1024]{1,0:T(8,128)(2,1)} dynamic-update-slice(bf16[512,1024]{1,0:T(8,128)(2,1)} %get-tuple-element.44, bf16[3,1024]{1,0:T(4,128)(2,1)S(1)} %fusion.20, s32[]{:T(128)} %constant.12.clone.1, s32[]{:T(128)} %constant.13.clone.1) | dynamic-update-slice | bytes 12292 | tf_op jit(solution)/shard_map/dynamic_update_slice | solution.py:600
  (69 shorter events, 1.0 us)
Async XLA Ops:
  0.6 11.9 %copy-start.18 = (f32[16]{0:T(128)S(1)}, f32[16]{0:T(128)}, u32[]{:S(2)}) copy-start(f32[16]{0:T(128)} %param.16) | copy-start | bytes 196
  2.1 10.7 %copy-start = (bf16[512,1024]{1,0:T(8,128)(2,1)S(1)}, bf16[512,1024]{1,0:T(8,128)(2,1)}, u32[]{:S(2)}) copy-start(bf16[512,1024]{1,0:T(8,128)(2,1)} %x_ref.3) | copy-start | bytes 3145732
  2.1 10.8 %copy-start.1 = (bf16[512,1024]{1,0:T(8,128)(2,1)S(1)}, bf16[512,1024]{1,0:T(8,128)(2,1)}, u32[]{:S(2)}) copy-start(bf16[512,1024]{1,0:T(8,128)(2,1)} %gy_ref.3) | copy-start | bytes 3145732
  2.1 10.8 %copy-start.2 = (f32[4,1024]{1,0:T(4,128)S(1)}, f32[4,1024]{1,0:T(4,128)}, u32[]{:S(2)}) copy-start(f32[4,1024]{1,0:T(4,128)} %taps_ref.3) | copy-start | bytes 49156
  2.1 10.8 %copy-start.3 = (f32[4,256]{1,0:T(4,128)S(1)}, f32[4,256]{1,0:T(4,128)}, u32[]{:S(2)}) copy-start(f32[4,256]{1,0:T(4,128)} %taps_bc_ref.1) | copy-start | bytes 12292
  2.1 10.6 %collective-permute-start = (bf16[3,1280]{1,0:T(4,128)(2,1)S(1)}, bf16[3,1280]{1,0:T(4,128)(2,1)S(1)}, u32[]{:S(2)}, u32[]{:S(2)}) collective-permute-start(bf16[3,1280]{1,0:T(4,128)(2,1)S(1)} %pad_maximum_fusion.3), channel_id=1, source_target_pairs={{0,4},{4,8},{8,12},{12,16},{16,20},{20,24},{24,28},{1,5},{5,9},{9,... | collective-permute-start | bytes 23048 | tf_op jit(solution)/shard_map/ppermute | solution.py:24
  8.3 4.2 %copy-start.16 = (f32[16]{0:T(128)}, f32[16]{0:T(128)S(1)}, u32[]{:S(2)}) copy-start(f32[16]{0:T(128)S(1)} %exp.14) | copy-start | bytes 196
  10.0 2.5 %copy-start.6 = (f32[512,16]{1,0:T(8,128)}, f32[512,16]{1,0:T(8,128)S(1)}, u32[]{:S(2)}) copy-start(f32[512,16]{1,0:T(8,128)S(1)} %get-tuple-element.70) | copy-start | bytes 98308
  10.0 2.5 %copy-start.4 = (f32[512,16]{1,0:T(8,128)}, f32[512,16]{1,0:T(8,128)S(1)}, u32[]{:S(2)}) copy-start(f32[512,16]{1,0:T(8,128)S(1)} %get-tuple-element.69) | copy-start | bytes 98308
  47.3 47.3 %copy-start.8 = (bf16[512,256]{1,0:T(8,128)(2,1)S(1)}, bf16[512,256]{1,0:T(8,128)(2,1)}, u32[]{:S(2)}) copy-start(bf16[512,256]{1,0:T(8,128)(2,1)} %param.10) | copy-start | bytes 786436
  47.3 47.3 %copy-start.9 = (f32[1,256]{1,0:T(1,128)S(1)}, f32[1,256]{1,0:T(1,128)}, u32[]{:S(2)}) copy-start(f32[1,256]{1,0:T(1,128)} %get-tuple-element.79) | copy-start | bytes 3076
  47.3 47.3 %copy-start.11 = (f32[1,256]{1,0:T(1,128)S(1)}, f32[1,256]{1,0:T(1,128)}, u32[]{:S(2)}) copy-start(f32[1,256]{1,0:T(1,128)} %get-tuple-element.80) | copy-start | bytes 3076
  47.3 47.3 %copy-start.13 = (f32[1,256]{1,0:T(1,128)S(1)}, f32[1,256]{1,0:T(1,128)}, u32[]{:S(2)}) copy-start(f32[1,256]{1,0:T(1,128)} %get-tuple-element.81) | copy-start | bytes 3076
  68.6 26.7 %copy-start.7 = (f32[512,16]{1,0:T(8,128)S(1)}, f32[512,16]{1,0:T(8,128)}, u32[]{:S(2)}) copy-start(f32[512,16]{1,0:T(8,128)} %copy-done.6) | copy-start | bytes 98308
  68.6 27.2 %copy-start.5 = (f32[512,16]{1,0:T(8,128)S(1)}, f32[512,16]{1,0:T(8,128)}, u32[]{:S(2)}) copy-start(f32[512,16]{1,0:T(8,128)} %copy-done.4) | copy-start | bytes 98308
  68.6 27.3 %copy-start.15 = (f32[16]{0:T(128)S(1)}, f32[16]{0:T(128)}, u32[]{:S(2)}) copy-start(f32[16]{0:T(128)} %param.14) | copy-start | bytes 196
  68.6 27.3 %copy-start.17 = (f32[16]{0:T(128)S(1)}, f32[16]{0:T(128)}, u32[]{:S(2)}) copy-start(f32[16]{0:T(128)} %copy-done.16) | copy-start | bytes 196
  95.2 14.8 %copy-start.10 = (f32[1,256]{1,0:T(1,128)S(1)}, f32[1,256]{1,0:T(1,128)}, u32[]{:S(2)}) copy-start(f32[1,256]{1,0:T(1,128)} %get-tuple-element.79) | copy-start | bytes 3076
  95.2 14.8 %copy-start.12 = (f32[1,256]{1,0:T(1,128)S(1)}, f32[1,256]{1,0:T(1,128)}, u32[]{:S(2)}) copy-start(f32[1,256]{1,0:T(1,128)} %get-tuple-element.80) | copy-start | bytes 3076
  95.2 14.7 %copy-start.14 = (f32[1,256]{1,0:T(1,128)S(1)}, f32[1,256]{1,0:T(1,128)}, u32[]{:S(2)}) copy-start(f32[1,256]{1,0:T(1,128)} %get-tuple-element.81) | copy-start | bytes 3076
  104.9 5.1 %collective-permute-start.1 = (f32[3,1280]{1,0:T(4,128)S(1)}, f32[3,1280]{1,0:T(4,128)S(1)}, u32[]{:S(2)}, u32[]{:S(2)}) collective-permute-start(f32[3,1280]{1,0:T(4,128)S(1)} %pad_maximum_fusion.2), channel_id=1, source_target_pairs={{4,0},{8,4},{12,8},{16,12},{20,16},{24,20},{28,24},{5,1},{9,5},{13... | collective-permute-start | bytes 46088 | tf_op jit(solution)/shard_map/ppermute | solution.py:24

commit v4 on v2

--- a/solution.py
+++ b/solution.py
@@ -135,8 +135,9 @@
     fout, fin, bout, bin_, fsend, frecv, bsend, brecv,
 ):
     me = lax.axis_index("seq")
-    chunks = ls_ref.shape[0]
-    lag = 2
+    chunks, rows, _ = ls_ref.shape
+    cut = chunks // dec_ref.shape[0]
+    lag = 4
     barrier = pltpu.get_barrier_semaphore()
 
     @pl.when(me > 0)
@@ -162,36 +163,40 @@
     def forward(k):
         @pl.when(me == 0)
         def _():
-            sin_ref[k] = jnp.zeros((N, LANES), F32)
+            sin_ref[k] = jnp.zeros((rows, LANES), F32)
             fout[k] = ls_ref[k]
 
         @pl.when(me > 0)
         def _():
             copy(fout, fin, fsend, frecv, k, me - 1).wait_recv()
-            got = fin[k]
-            sin_ref[k] = got
-            fout[k] = dec_ref[k][0:1, :] * got + ls_ref[k]
+            fout[k] = dec_ref[k // cut][0:1, :] * fin[k] + ls_ref[k]
 
         @pl.when(me < size - 1)
         def _():
             copy(fout, fin, fsend, frecv, k, me + 1).start()
+
+        @pl.when(me > 0)
+        def _():
+            sin_ref[k] = fin[k]
 
     def backward(k):
         @pl.when(me == size - 1)
         def _():
-            gin_ref[k] = jnp.zeros((N, LANES), F32)
+            gin_ref[k] = jnp.zeros((rows, LANES), F32)
             bout[k] = lg_ref[k]
 
         @pl.when(me < size - 1)
         def _():
             copy(bout, bin_, bsend, brecv, k, me + 1).wait_recv()
-            got = bin_[k]
-            gin_ref[k] = got
-            bout[k] = dec_ref[k][0:1, :] * got + lg_ref[k]
+            bout[k] = dec_ref[k // cut][0:1, :] * bin_[k] + lg_ref[k]
 
         @pl.when(me > 0)
         def _():
             copy(bout, bin_, bsend, brecv, k, me - 1).start()
+
+        @pl.when(me < size - 1)
+        def _():
+            gin_ref[k] = bin_[k]
 
     late_f = lax.max(0, 2 * me - (size - 1)) * lag
     late_b = lax.max(0, (size - 1) - 2 * me) * lag
@@ -496,18 +501,21 @@
     )(x_halo, x_raw, d_out, conv_x, bc_ext, conv_bc, s_pad, la_pad)
 
     in_vmem = pl.BlockSpec(memory_space=pltpu.VMEM)
+    pieces = (pairs * 2, N // 2, LANES)
     state_in, grad_in = pl.pallas_call(
         lambda *refs: chain_kernel(size, *refs),
         in_specs=[in_vmem] * 3,
         out_specs=[in_vmem] * 2,
-        out_shape=[shape((pairs, N, LANES), F32)] * 2,
-        scratch_shapes=[pltpu.VMEM((pairs, N, LANES), F32)] * 4
-        + [pltpu.SemaphoreType.DMA((pairs,))] * 4,
+        out_shape=[shape(pieces, F32)] * 2,
+        scratch_shapes=[pltpu.VMEM(pieces, F32)] * 4
+        + [pltpu.SemaphoreType.DMA((pieces[0],))] * 4,
         compiler_params=pltpu.CompilerParams(
             collective_id=0, has_side_effects=True, vmem_limit_bytes=VMEM_LIMIT
         ),
         name="chain",
-    )(ls, lg, dec)
+    )(ls.reshape(pieces), lg.reshape(pieces), dec)
+    state_in = state_in.reshape(pairs, N, LANES)
+    grad_in = grad_in.reshape(pairs, N, LANES)
 
     layer_out, grad_x, tail, first, tap_grad, skip_grad, bc_local, u, v, bnd = pl.pallas_call(
         main_kernel,

time: 111 us -> 110 us (level)
  no operation moved by 1% of the time
where the time goes in v4:
time: 110 us
  Pallas kernels  87.3 us (79%)
  local copies, waits for them, and re-layouts  9.8 us (9%)
  starting transfers between devices  6.14 us (6%)
  other arithmetic  3.84 us (3%)
  waiting for transfers between devices  1.14 us (1%)
    pallas_call x1, Pallas kernels, local(): pl.pallas_call(lambda *refs: head_sum_kernel(heads, *refs), in_specs=[in_...  28.5 us
    pallas_call x1, Pallas kernels, local(): pl.pallas_call(main_kernel, grid=(pairs,), in_specs=[columns(8), columns(...  21.3 us
    pallas_call x1, Pallas kernels, local(): pl.pallas_call(lambda *refs: chain_kernel(size, *refs), in_specs=[in_vmem...  19.3 us
    pallas_call x1, Pallas kernels, local(): pl.pallas_call(terms_kernel, grid=(pairs,), in_specs=[columns(8), columns...  10.2 us
    pallas_call x1, Pallas kernels, local(): pl.pallas_call(lambda *refs: share_kernel(size, *refs), in_specs=[in_vmem...  8.12 us
    ppermute x2, starting transfers between devices, shifted(): return lax.ppermute(block, axis, route)  6.14 us
  transfers between devices with their start and end apart: 2, of which 1 were waited for; matrix products, arithmetic and copies ran while one was open for 8% of the time, Pallas kernels for 0%

profile of v4, /device:TPU:27, one launch (start us, length us, event | category | flops | bytes accessed | tf_op | source)
XLA Modules:
  0.0 109.6 jit_solution(16207710843495949027)
XLA Ops:
  0.7 0.7 slice.109
  1.4 0.7 slice.110
  2.1 3.8 %collective-permute-start = (bf16[3,1280]{1,0:T(4,128)(2,1)S(1)}, bf16[3,1280]{1,0:T(4,128)(2,1)S(1)}, u32[]{:S(2)}, u32[]{:S(2)}) collective-permute-start(bf16[3,1280]{1,0:T(4,128)(2,1)S(1)} %pad_maximum_fusion.3), channel_id=1, source_target_pairs={{0,4},{4,8},{8,12},{12,16},{16,20},{20,24},{24,28},{1,5},{5,9},{9,... | collective-permute-start | bytes 23048 | tf_op jit(solution)/shard_map/ppermute | solution.py:24
  5.9 0.9 copy.18
  6.8 0.7 exp.14
  7.5 0.8 fusion.25
  8.3 0.8 negate_multiply_fusion
  9.2 1.5 %fusion.26 = (f32[1,256]{1,0:T(1,128)S(1)}, f32[1,256]{1,0:T(1,128)}, f32[1,256]{1,0:T(1,128)}, f32[1,256]{1,0:T(1,128)}) fusion(f32[4,256]{1,0:T(4,128)} %taps_bc_ref.1), kind=kLoop, calls=%fused_computation.53 | loop fusion | bytes 8192 | tf_op jit(solution)/shard_map/slice | solution.py:567
  10.7 1.0 convert_element_type.17
  12.0 10.2 %terms.1 = (f32[8,4,128,128]{3,2,1,0:T(8,128)S(1)}, f32[8,4,128,128]{3,2,1,0:T(8,128)S(1)}, f32[8,128,128]{2,1,0:T(8,128)S(1)}, f32[8,128,128]{2,1,0:T(8,128)S(1...) custom-call(f32[8,1024]{1,0:T(8,128)S(1)} %slice.142.halo_ref, ...), custom_call_target="tpu_custom_call" | custom-call | tf_op jit(solution)/shard_map/terms/pallas_call | solution.py:478
  22.2 19.3 %chain.1 = (f32[16,64,128]{2,1,0:T(8,128)S(1)}, f32[16,64,128]{2,1,0:T(8,128)S(1)}) custom-call(f32[16,64,128]{2,1,0:T(8,128)S(1)} %bitcast.45, f32[16,64,128]{2,1,0:T(8,128)S(1)} %bitcast.46, f32[8,8,128]{2,1,0:T(8,128)S(1)} %get-tuple-element.40.refs_2_), custom_call_target="tpu_custom_call" | custom-call | tf_op jit(solution)/shard_map/chain/pallas_call | solution.py:505
  41.6 21.3 %main.1 = (bf16[512,1024]{1,0:T(8,128)(2,1)}, bf16[512,1024]{1,0:T(8,128)(2,1)}, f32[8,1024]{1,0:T(8,128)S(1)}, f32[8,1024]{1,0:T(8,128)S(1)}, f32[4,1024]{1,0:T...) custom-call(f32[8,1024]{1,0:T(8,128)S(1)} %slice.142.halo_ref, ...), custom_call_target="tpu_custom_call" | custom-call | tf_op jit(solution)/shard_map/main/pallas_call | solution.py:520
  62.8 28.5 %head_sum.1 = f32[512,256]{1,0:T(8,128)S(1)} custom-call(f32[512,256]{1,0:T(8,128)S(1)} %get-tuple-element.47.refs_0_), custom_call_target="tpu_custom_call" | custom-call | tf_op jit(solution)/shard_map/head_sum/pallas_call | solution.py:554
  91.4 0.6 multiply_reduce_fusion.3
  92.1 0.3 fusion
  93.1 8.1 %share.1 = f32[48,128]{1,0:T(8,128)S(1)} custom-call(f32[48,128]{1,0:T(8,128)S(1)} %pad_bitcast_fusion.refs_0_), custom_call_target="tpu_custom_call" | custom-call | tf_op jit(solution)/shard_map/share/pallas_call | solution.py:605
  101.2 2.3 %collective-permute-start.1 = (f32[3,1280]{1,0:T(4,128)S(1)}, f32[3,1280]{1,0:T(4,128)S(1)}, u32[]{:S(2)}, u32[]{:S(2)}) collective-permute-start(f32[3,1280]{1,0:T(4,128)S(1)} %pad_maximum_fusion.2), channel_id=1, source_target_pairs={{4,0},{8,4},{12,8},{16,12},{20,16},{24,20},{28,24},{5,1},{9,5},{13... | collective-permute-start | bytes 46088 | tf_op jit(solution)/shard_map/ppermute | solution.py:24
  103.6 0.6 fusion.24
  104.1 0.6 reshape.70
  104.8 0.6 reshape.71
  105.4 0.7 copy.21
  106.1 1.1 %collective-permute-done.1 = f32[3,1280]{1,0:T(4,128)S(1)} collective-permute-done((f32[3,1280]{1,0:T(4,128)S(1)}, f32[3,1280]{1,0:T(4,128)S(1)}, u32[]{:S(2)}, u32[]{:S(2)}) %collective-permute-start.1) | collective-permute-done | bytes 15392 | tf_op jit(solution)/shard_map/ppermute | solution.py:24
  107.2 1.0 fusion.5
  108.3 1.4 %dynamic_update_slice.3 = bf16[512,1024]{1,0:T(8,128)(2,1)} dynamic-update-slice(bf16[512,1024]{1,0:T(8,128)(2,1)} %get-tuple-element.44, bf16[3,1024]{1,0:T(4,128)(2,1)S(1)} %fusion.20, s32[]{:T(128)} %constant.12.clone.1, s32[]{:T(128)} %constant.13.clone.1) | dynamic-update-slice | bytes 12292 | tf_op jit(solution)/shard_map/dynamic_update_slice | solution.py:584
  (69 shorter events, 1.0 us)
Async XLA Ops:
  0.6 11.1 %copy-start.18 = (f32[16]{0:T(128)S(1)}, f32[16]{0:T(128)}, u32[]{:S(2)}) copy-start(f32[16]{0:T(128)} %param.16) | copy-start | bytes 196
  2.1 9.9 %copy-start = (bf16[512,1024]{1,0:T(8,128)(2,1)S(1)}, bf16[512,1024]{1,0:T(8,128)(2,1)}, u32[]{:S(2)}) copy-start(bf16[512,1024]{1,0:T(8,128)(2,1)} %x_ref.3) | copy-start | bytes 3145732
  2.1 9.9 %copy-start.1 = (bf16[512,1024]{1,0:T(8,128)(2,1)S(1)}, bf16[512,1024]{1,0:T(8,128)(2,1)}, u32[]{:S(2)}) copy-start(bf16[512,1024]{1,0:T(8,128)(2,1)} %gy_ref.3) | copy-start | bytes 3145732
  2.1 9.9 %copy-start.2 = (f32[4,1024]{1,0:T(4,128)S(1)}, f32[4,1024]{1,0:T(4,128)}, u32[]{:S(2)}) copy-start(f32[4,1024]{1,0:T(4,128)} %taps_ref.3) | copy-start | bytes 49156
  2.1 9.9 %copy-start.3 = (f32[4,256]{1,0:T(4,128)S(1)}, f32[4,256]{1,0:T(4,128)}, u32[]{:S(2)}) copy-start(f32[4,256]{1,0:T(4,128)} %taps_bc_ref.1) | copy-start | bytes 12292
  2.1 9.8 %collective-permute-start = (bf16[3,1280]{1,0:T(4,128)(2,1)S(1)}, bf16[3,1280]{1,0:T(4,128)(2,1)S(1)}, u32[]{:S(2)}, u32[]{:S(2)}) collective-permute-start(bf16[3,1280]{1,0:T(4,128)(2,1)S(1)} %pad_maximum_fusion.3), channel_id=1, source_target_pairs={{0,4},{4,8},{8,12},{12,16},{16,20},{20,24},{24,28},{1,5},{5,9},{9,... | collective-permute-start | bytes 23048 | tf_op jit(solution)/shard_map/ppermute | solution.py:24
  7.5 4.2 %copy-start.16 = (f32[16]{0:T(128)}, f32[16]{0:T(128)S(1)}, u32[]{:S(2)}) copy-start(f32[16]{0:T(128)S(1)} %exp.14) | copy-start | bytes 196
  9.2 2.5 %copy-start.6 = (f32[512,16]{1,0:T(8,128)}, f32[512,16]{1,0:T(8,128)S(1)}, u32[]{:S(2)}) copy-start(f32[512,16]{1,0:T(8,128)S(1)} %get-tuple-element.70) | copy-start | bytes 98308
  9.2 2.5 %copy-start.4 = (f32[512,16]{1,0:T(8,128)}, f32[512,16]{1,0:T(8,128)S(1)}, u32[]{:S(2)}) copy-start(f32[512,16]{1,0:T(8,128)S(1)} %get-tuple-element.69) | copy-start | bytes 98308
  41.5 49.8 %copy-start.8 = (bf16[512,256]{1,0:T(8,128)(2,1)S(1)}, bf16[512,256]{1,0:T(8,128)(2,1)}, u32[]{:S(2)}) copy-start(bf16[512,256]{1,0:T(8,128)(2,1)} %param.10) | copy-start | bytes 786436
  41.5 49.8 %copy-start.9 = (f32[1,256]{1,0:T(1,128)S(1)}, f32[1,256]{1,0:T(1,128)}, u32[]{:S(2)}) copy-start(f32[1,256]{1,0:T(1,128)} %get-tuple-element.79) | copy-start | bytes 3076
  41.5 49.8 %copy-start.11 = (f32[1,256]{1,0:T(1,128)S(1)}, f32[1,256]{1,0:T(1,128)}, u32[]{:S(2)}) copy-start(f32[1,256]{1,0:T(1,128)} %get-tuple-element.80) | copy-start | bytes 3076
  41.5 49.8 %copy-start.13 = (f32[1,256]{1,0:T(1,128)S(1)}, f32[1,256]{1,0:T(1,128)}, u32[]{:S(2)}) copy-start(f32[1,256]{1,0:T(1,128)} %get-tuple-element.81) | copy-start | bytes 3076
  62.8 29.2 %copy-start.7 = (f32[512,16]{1,0:T(8,128)S(1)}, f32[512,16]{1,0:T(8,128)}, u32[]{:S(2)}) copy-start(f32[512,16]{1,0:T(8,128)} %copy-done.6) | copy-start | bytes 98308
  62.8 29.8 %copy-start.5 = (f32[512,16]{1,0:T(8,128)S(1)}, f32[512,16]{1,0:T(8,128)}, u32[]{:S(2)}) copy-start(f32[512,16]{1,0:T(8,128)} %copy-done.4) | copy-start | bytes 98308
  62.8 29.8 %copy-start.15 = (f32[16]{0:T(128)S(1)}, f32[16]{0:T(128)}, u32[]{:S(2)}) copy-start(f32[16]{0:T(128)} %param.14) | copy-start | bytes 196
  62.8 29.8 %copy-start.17 = (f32[16]{0:T(128)S(1)}, f32[16]{0:T(128)}, u32[]{:S(2)}) copy-start(f32[16]{0:T(128)} %copy-done.16) | copy-start | bytes 196
  92.0 15.3 %copy-start.10 = (f32[1,256]{1,0:T(1,128)S(1)}, f32[1,256]{1,0:T(1,128)}, u32[]{:S(2)}) copy-start(f32[1,256]{1,0:T(1,128)} %get-tuple-element.79) | copy-start | bytes 3076
  92.0 15.3 %copy-start.12 = (f32[1,256]{1,0:T(1,128)S(1)}, f32[1,256]{1,0:T(1,128)}, u32[]{:S(2)}) copy-start(f32[1,256]{1,0:T(1,128)} %get-tuple-element.80) | copy-start | bytes 3076
  92.0 15.3 %copy-start.14 = (f32[1,256]{1,0:T(1,128)S(1)}, f32[1,256]{1,0:T(1,128)}, u32[]{:S(2)}) copy-start(f32[1,256]{1,0:T(1,128)} %get-tuple-element.81) | copy-start | bytes 3076
  101.2 6.0 %collective-permute-start.1 = (f32[3,1280]{1,0:T(4,128)S(1)}, f32[3,1280]{1,0:T(4,128)S(1)}, u32[]{:S(2)}, u32[]{:S(2)}) collective-permute-start(f32[3,1280]{1,0:T(4,128)S(1)} %pad_maximum_fusion.2), channel_id=1, source_target_pairs={{4,0},{8,4},{12,8},{16,12},{20,16},{24,20},{28,24},{5,1},{9,5},{13... | collective-permute-start | bytes 46088 | tf_op jit(solution)/shard_map/ppermute | solution.py:24

commit v5 on v4

--- a/solution.py
+++ b/solution.py
@@ -272,49 +272,54 @@
     me = lax.axis_index("head")
     greet("head", size, me)
     rows = in_ref.shape[0] // size
-
-    def block(i):
-        return pl.ds(pl.multiple_of(i * rows, rows), rows)
-
-    def scatter(d, owner, target):
+    parts = 2
+    part = rows // parts
+
+    def block(i, h):
+        return pl.ds(pl.multiple_of(i * rows + h * part, part), part)
+
+    def scatter(d, h, owner, target):
         return pltpu.make_async_remote_copy(
-            src_ref=in_ref.at[block(target)],
-            dst_ref=got.at[owner],
-            send_sem=send1.at[d],
-            recv_sem=recv1.at[owner],
+            src_ref=in_ref.at[block(target, h)],
+            dst_ref=got.at[owner, pl.ds(h * part, part)],
+            send_sem=send1.at[h, d],
+            recv_sem=recv1.at[h, owner],
             device_id={"head": target},
             device_id_type=MESH,
         )
 
-    def gather(d, owner, target):
+    def gather(d, h, owner, target):
         return pltpu.make_async_remote_copy(
-            src_ref=out_ref.at[block(owner)],
-            dst_ref=out_ref.at[block(owner)],
-            send_sem=send2.at[d],
-            recv_sem=recv2.at[owner],
+            src_ref=out_ref.at[block(owner, h)],
+            dst_ref=out_ref.at[block(owner, h)],
+            send_sem=send2.at[h, d],
+            recv_sem=recv2.at[h, owner],
             device_id={"head": target},
             device_id_type=MESH,
         )
 
-    for d in range(1, size):
-        scatter(d, me, lax.rem(me + d, size)).start()
-    got[me] = in_ref[block(me), :]
-    for d in range(1, size):
-        source = lax.rem(me + size - d, size)
-        scatter(d, source, source).wait_recv()
-    total = got[0]
-    for i in range(1, size):
-        total = total + got[i]
-    out_ref[block(me), :] = total
-    for d in range(1, size):
-        gather(d, me, lax.rem(me + d, size)).start()
-    for d in range(1, size):
-        source = lax.rem(me + size - d, size)
-        gather(d, source, source).wait_recv()
-    for d in range(1, size):
-        target = lax.rem(me + d, size)
-        scatter(d, me, target).wait_send()
-        gather(d, me, target).wait_send()
+    for h in range(parts):
+        for d in range(1, size):
+            scatter(d, h, me, lax.rem(me + d, size)).start()
+    for h in range(parts):
+        got[me, h * part : (h + 1) * part] = in_ref[block(me, h), :]
+        for d in range(1, size):
+            source = lax.rem(me + size - d, size)
+            scatter(d, h, source, source).wait_recv()
+        total = got[0, h * part : (h + 1) * part]
+        for i in range(1, size):
+            total = total + got[i, h * part : (h + 1) * part]
+        out_ref[block(me, h), :] = total
+        for d in range(1, size):
+            gather(d, h, me, lax.rem(me + d, size)).start()
+    for h in range(parts):
+        for d in range(1, size):
+            source = lax.rem(me + size - d, size)
+            gather(d, h, source, source).wait_recv()
+        for d in range(1, size):
+            target = lax.rem(me + d, size)
+            scatter(d, h, me, target).wait_send()
+            gather(d, h, me, target).wait_send()
 
 
 def main_kernel(
@@ -557,7 +562,7 @@
         out_specs=in_vmem,
         out_shape=shape((frames, 2 * N), F32),
         scratch_shapes=[pltpu.VMEM((heads, frames // heads, 2 * N), F32)]
-        + [pltpu.SemaphoreType.DMA((heads,))] * 4,
+        + [pltpu.SemaphoreType.DMA((2, heads))] * 4,
         compiler_params=pltpu.CompilerParams(
             collective_id=1, has_side_effects=True, vmem_limit_bytes=VMEM_LIMIT
         ),

time: 110 us -> 109 us (level)
  Pallas kernels: 87.3 us -> 86.1 us
    pallas_call x1, Pallas kernels: 28.5 us -> 24.7 us  [local(): pl.pallas_call(lambda *refs: head_sum_kernel(heads, *refs), in_specs=[in_...]
    pallas_call x1, Pallas kernels: 8.12 us -> 10.7 us  [local(): pl.pallas_call(lambda *refs: share_kernel(size, *refs), in_specs=[in_vmem...]
where the time goes in v5:
time: 109 us; the launch traced here: 108 us
  Pallas kernels  86.1 us (79%)
  local copies, waits for them, and re-layouts  9.8 us (9%)
  starting transfers between devices  6.14 us (6%)
  other arithmetic  3.84 us (4%)
  waiting for transfers between devices  1.14 us (1%)
    pallas_call x1, Pallas kernels, local(): pl.pallas_call(lambda *refs: head_sum_kernel(heads, *refs), in_specs=[in_...  24.7 us
    pallas_call x1, Pallas kernels, local(): pl.pallas_call(main_kernel, grid=(pairs,), in_specs=[columns(8), columns(...  21.3 us
    pallas_call x1, Pallas kernels, local(): pl.pallas_call(lambda *refs: chain_kernel(size, *refs), in_specs=[in_vmem...  19.3 us
    pallas_call x1, Pallas kernels, local(): pl.pallas_call(lambda *refs: share_kernel(size, *refs), in_specs=[in_vmem...  10.7 us
    pallas_call x1, Pallas kernels, local(): pl.pallas_call(terms_kernel, grid=(pairs,), in_specs=[columns(8), columns...  10.2 us
    ppermute x2, starting transfers between devices, shifted(): return lax.ppermute(block, axis, route)  6.14 us
  transfers between devices with their start and end apart: 2, of which 1 were waited for; matrix products, arithmetic and copies ran while one was open for 8% of the time, Pallas kernels for 0%

profile of v5, /device:TPU:27, one launch (start us, length us, event | category | flops | bytes accessed | tf_op | source)
XLA Modules:
  0.0 108.4 jit_solution(14830361527570576149)
XLA Ops:
  0.7 0.7 slice.109
  1.4 0.7 slice.110
  2.1 3.8 %collective-permute-start = (bf16[3,1280]{1,0:T(4,128)(2,1)S(1)}, bf16[3,1280]{1,0:T(4,128)(2,1)S(1)}, u32[]{:S(2)}, u32[]{:S(2)}) collective-permute-start(bf16[3,1280]{1,0:T(4,128)(2,1)S(1)} %pad_maximum_fusion.3), channel_id=1, source_target_pairs={{0,4},{4,8},{8,12},{12,16},{16,20},{20,24},{24,28},{1,5},{5,9},{9,... | collective-permute-start | bytes 23048 | tf_op jit(solution)/shard_map/ppermute | solution.py:24
  5.9 0.9 copy.18
  6.8 0.7 exp.14
  7.5 0.8 fusion.25
  8.3 0.8 negate_multiply_fusion
  9.2 1.5 %fusion.26 = (f32[1,256]{1,0:T(1,128)S(1)}, f32[1,256]{1,0:T(1,128)}, f32[1,256]{1,0:T(1,128)}, f32[1,256]{1,0:T(1,128)}) fusion(f32[4,256]{1,0:T(4,128)} %taps_bc_ref.1), kind=kLoop, calls=%fused_computation.53 | loop fusion | bytes 8192 | tf_op jit(solution)/shard_map/slice | solution.py:572
  10.7 1.0 convert_element_type.17
  12.0 10.2 %terms.1 = (f32[8,4,128,128]{3,2,1,0:T(8,128)S(1)}, f32[8,4,128,128]{3,2,1,0:T(8,128)S(1)}, f32[8,128,128]{2,1,0:T(8,128)S(1)}, f32[8,128,128]{2,1,0:T(8,128)S(1...) custom-call(f32[8,1024]{1,0:T(8,128)S(1)} %slice.142.halo_ref, ...), custom_call_target="tpu_custom_call" | custom-call | tf_op jit(solution)/shard_map/terms/pallas_call | solution.py:483
  22.2 19.3 %chain.1 = (f32[16,64,128]{2,1,0:T(8,128)S(1)}, f32[16,64,128]{2,1,0:T(8,128)S(1)}) custom-call(f32[16,64,128]{2,1,0:T(8,128)S(1)} %bitcast.45, f32[16,64,128]{2,1,0:T(8,128)S(1)} %bitcast.46, f32[8,8,128]{2,1,0:T(8,128)S(1)} %get-tuple-element.40.refs_2_), custom_call_target="tpu_custom_call" | custom-call | tf_op jit(solution)/shard_map/chain/pallas_call | solution.py:510
  41.6 21.3 %main.1 = (bf16[512,1024]{1,0:T(8,128)(2,1)}, bf16[512,1024]{1,0:T(8,128)(2,1)}, f32[8,1024]{1,0:T(8,128)S(1)}, f32[8,1024]{1,0:T(8,128)S(1)}, f32[4,1024]{1,0:T...) custom-call(f32[8,1024]{1,0:T(8,128)S(1)} %slice.142.halo_ref, ...), custom_call_target="tpu_custom_call" | custom-call | tf_op jit(solution)/shard_map/main/pallas_call | solution.py:525
  62.8 24.7 %head_sum.1 = f32[512,256]{1,0:T(8,128)S(1)} custom-call(f32[512,256]{1,0:T(8,128)S(1)} %get-tuple-element.47.refs_0_), custom_call_target="tpu_custom_call" | custom-call | tf_op jit(solution)/shard_map/head_sum/pallas_call | solution.py:559
  87.6 0.6 multiply_reduce_fusion.3
  88.3 0.3 fusion
  89.3 10.7 %share.1 = f32[48,128]{1,0:T(8,128)S(1)} custom-call(f32[48,128]{1,0:T(8,128)S(1)} %pad_bitcast_fusion.refs_0_), custom_call_target="tpu_custom_call" | custom-call | tf_op jit(solution)/shard_map/share/pallas_call | solution.py:610
  100.0 2.3 %collective-permute-start.1 = (f32[3,1280]{1,0:T(4,128)S(1)}, f32[3,1280]{1,0:T(4,128)S(1)}, u32[]{:S(2)}, u32[]{:S(2)}) collective-permute-start(f32[3,1280]{1,0:T(4,128)S(1)} %pad_maximum_fusion.2), channel_id=1, source_target_pairs={{4,0},{8,4},{12,8},{16,12},{20,16},{24,20},{28,24},{5,1},{9,5},{13... | collective-permute-start | bytes 46088 | tf_op jit(solution)/shard_map/ppermute | solution.py:24
  102.3 0.6 fusion.24
  102.9 0.6 reshape.70
  103.5 0.6 reshape.71
  104.1 0.7 copy.21
  104.8 1.1 %collective-permute-done.1 = f32[3,1280]{1,0:T(4,128)S(1)} collective-permute-done((f32[3,1280]{1,0:T(4,128)S(1)}, f32[3,1280]{1,0:T(4,128)S(1)}, u32[]{:S(2)}, u32[]{:S(2)}) %collective-permute-start.1) | collective-permute-done | bytes 15392 | tf_op jit(solution)/shard_map/ppermute | solution.py:24
  106.0 1.0 fusion.5
  107.0 1.4 %dynamic_update_slice.3 = bf16[512,1024]{1,0:T(8,128)(2,1)} dynamic-update-slice(bf16[512,1024]{1,0:T(8,128)(2,1)} %get-tuple-element.44, bf16[3,1024]{1,0:T(4,128)(2,1)S(1)} %fusion.20, s32[]{:T(128)} %constant.12.clone.1, s32[]{:T(128)} %constant.13.clone.1) | dynamic-update-slice | bytes 12292 | tf_op jit(solution)/shard_map/dynamic_update_slice | solution.py:589
  (69 shorter events, 1.0 us)
Async XLA Ops:
  0.6 11.1 %copy-start.18 = (f32[16]{0:T(128)S(1)}, f32[16]{0:T(128)}, u32[]{:S(2)}) copy-start(f32[16]{0:T(128)} %param.16) | copy-start | bytes 196
  2.1 9.9 %copy-start = (bf16[512,1024]{1,0:T(8,128)(2,1)S(1)}, bf16[512,1024]{1,0:T(8,128)(2,1)}, u32[]{:S(2)}) copy-start(bf16[512,1024]{1,0:T(8,128)(2,1)} %x_ref.3) | copy-start | bytes 3145732
  2.1 9.9 %copy-start.1 = (bf16[512,1024]{1,0:T(8,128)(2,1)S(1)}, bf16[512,1024]{1,0:T(8,128)(2,1)}, u32[]{:S(2)}) copy-start(bf16[512,1024]{1,0:T(8,128)(2,1)} %gy_ref.3) | copy-start | bytes 3145732
  2.1 9.9 %copy-start.2 = (f32[4,1024]{1,0:T(4,128)S(1)}, f32[4,1024]{1,0:T(4,128)}, u32[]{:S(2)}) copy-start(f32[4,1024]{1,0:T(4,128)} %taps_ref.3) | copy-start | bytes 49156
  2.1 9.9 %copy-start.3 = (f32[4,256]{1,0:T(4,128)S(1)}, f32[4,256]{1,0:T(4,128)}, u32[]{:S(2)}) copy-start(f32[4,256]{1,0:T(4,128)} %taps_bc_ref.1) | copy-start | bytes 12292
  2.1 9.8 %collective-permute-start = (bf16[3,1280]{1,0:T(4,128)(2,1)S(1)}, bf16[3,1280]{1,0:T(4,128)(2,1)S(1)}, u32[]{:S(2)}, u32[]{:S(2)}) collective-permute-start(bf16[3,1280]{1,0:T(4,128)(2,1)S(1)} %pad_maximum_fusion.3), channel_id=1, source_target_pairs={{0,4},{4,8},{8,12},{12,16},{16,20},{20,24},{24,28},{1,5},{5,9},{9,... | collective-permute-start | bytes 23048 | tf_op jit(solution)/shard_map/ppermute | solution.py:24
  7.5 4.2 %copy-start.16 = (f32[16]{0:T(128)}, f32[16]{0:T(128)S(1)}, u32[]{:S(2)}) copy-start(f32[16]{0:T(128)S(1)} %exp.14) | copy-start | bytes 196
  9.2 2.5 %copy-start.6 = (f32[512,16]{1,0:T(8,128)}, f32[512,16]{1,0:T(8,128)S(1)}, u32[]{:S(2)}) copy-start(f32[512,16]{1,0:T(8,128)S(1)} %get-tuple-element.70) | copy-start | bytes 98308
  9.2 2.5 %copy-start.4 = (f32[512,16]{1,0:T(8,128)}, f32[512,16]{1,0:T(8,128)S(1)}, u32[]{:S(2)}) copy-start(f32[512,16]{1,0:T(8,128)S(1)} %get-tuple-element.69) | copy-start | bytes 98308
  41.5 46.0 %copy-start.8 = (bf16[512,256]{1,0:T(8,128)(2,1)S(1)}, bf16[512,256]{1,0:T(8,128)(2,1)}, u32[]{:S(2)}) copy-start(bf16[512,256]{1,0:T(8,128)(2,1)} %param.10) | copy-start | bytes 786436
  41.5 46.0 %copy-start.9 = (f32[1,256]{1,0:T(1,128)S(1)}, f32[1,256]{1,0:T(1,128)}, u32[]{:S(2)}) copy-start(f32[1,256]{1,0:T(1,128)} %get-tuple-element.79) | copy-start | bytes 3076
  41.5 46.0 %copy-start.11 = (f32[1,256]{1,0:T(1,128)S(1)}, f32[1,256]{1,0:T(1,128)}, u32[]{:S(2)}) copy-start(f32[1,256]{1,0:T(1,128)} %get-tuple-element.80) | copy-start | bytes 3076
  41.5 46.0 %copy-start.13 = (f32[1,256]{1,0:T(1,128)S(1)}, f32[1,256]{1,0:T(1,128)}, u32[]{:S(2)}) copy-start(f32[1,256]{1,0:T(1,128)} %get-tuple-element.81) | copy-start | bytes 3076
  62.8 25.4 %copy-start.7 = (f32[512,16]{1,0:T(8,128)S(1)}, f32[512,16]{1,0:T(8,128)}, u32[]{:S(2)}) copy-start(f32[512,16]{1,0:T(8,128)} %copy-done.6) | copy-start | bytes 98308
  62.8 26.0 %copy-start.5 = (f32[512,16]{1,0:T(8,128)S(1)}, f32[512,16]{1,0:T(8,128)}, u32[]{:S(2)}) copy-start(f32[512,16]{1,0:T(8,128)} %copy-done.4) | copy-start | bytes 98308
  62.8 26.0 %copy-start.15 = (f32[16]{0:T(128)S(1)}, f32[16]{0:T(128)}, u32[]{:S(2)}) copy-start(f32[16]{0:T(128)} %param.14) | copy-start | bytes 196
  62.8 26.0 %copy-start.17 = (f32[16]{0:T(128)S(1)}, f32[16]{0:T(128)}, u32[]{:S(2)}) copy-start(f32[16]{0:T(128)} %copy-done.16) | copy-start | bytes 196
  88.2 17.8 %copy-start.10 = (f32[1,256]{1,0:T(1,128)S(1)}, f32[1,256]{1,0:T(1,128)}, u32[]{:S(2)}) copy-start(f32[1,256]{1,0:T(1,128)} %get-tuple-element.79) | copy-start | bytes 3076
  88.2 17.8 %copy-start.12 = (f32[1,256]{1,0:T(1,128)S(1)}, f32[1,256]{1,0:T(1,128)}, u32[]{:S(2)}) copy-start(f32[1,256]{1,0:T(1,128)} %get-tuple-element.80) | copy-start | bytes 3076
  88.2 17.8 %copy-start.14 = (f32[1,256]{1,0:T(1,128)S(1)}, f32[1,256]{1,0:T(1,128)}, u32[]{:S(2)}) copy-start(f32[1,256]{1,0:T(1,128)} %get-tuple-element.81) | copy-start | bytes 3076
  100.0 6.0 %collective-permute-start.1 = (f32[3,1280]{1,0:T(4,128)S(1)}, f32[3,1280]{1,0:T(4,128)S(1)}, u32[]{:S(2)}, u32[]{:S(2)}) collective-permute-start(f32[3,1280]{1,0:T(4,128)S(1)} %pad_maximum_fusion.2), channel_id=1, source_target_pairs={{4,0},{8,4},{12,8},{16,12},{20,16},{24,20},{28,24},{5,1},{9,5},{13... | collective-permute-start | bytes 46088 | tf_op jit(solution)/shard_map/ppermute | solution.py:24
